TPU v7x, 32 devices: a whole 2x2x4 slice. The times are simulated.
32 devices in a mesh: dp: 2 (over y), seq: 4 (over z), mp: 4 (over x, core).
Axes of the slice: x: 2, y: 2, z: 4, core: 2. Of those that a mesh axis runs over, the one named last changes fastest.
Arguments:
- hidden_in: bfloat16 [4, 4096, 768], P('dp', 'seq'), may hold values from -6 to 6
- segments: int32 [4, 4096], P('dp', 'seq'), may hold values from 0 to 3, as said below
- cotangent: bfloat16 [4, 4096, 768], P('dp', 'seq'), may hold values from -6 to 6
- qkv_weight: bfloat16 [768, 3, 768], P(('dp', 'seq'), None, 'mp'), may hold values from -0.21875 to 0.21875
- qv_bias: float32 [2, 768], P(None, 'mp'), may hold values from -3 to 3
- proj_weight: bfloat16 [768, 768], P(('dp', 'seq'), 'mp'), may hold values from -0.875 to 0.875
- proj_bias: float32 [768], replicated, may hold values from -2 to 2
- first_gain: float32 [768], replicated, may hold values from 0.5 to 1.5
- first_shift: float32 [768], replicated, may hold values from -2 to 2
- up_weight: bfloat16 [768, 3072], P(('dp', 'seq'), 'mp'), may hold values from -0.21875 to 0.21875
- up_bias: float32 [3072], P('mp'), may hold values from -3 to 3
- down_weight: bfloat16 [768, 3072], P(('dp', 'seq'), 'mp'), may hold values from -0.109375 to 0.109375
- down_bias: float32 [768], replicated, may hold values from -2 to 2
- second_gain: float32 [768], replicated, may hold values from 0.5 to 1.5
- second_shift: float32 [768], replicated, may hold values from -2 to 2
Outputs:
- layer_out: bfloat16 [4, 4096, 768], P('dp', 'seq')
- input_grad: float32 [4, 4096, 768], P('dp', 'seq')
- qkv_grad: float32 [768, 3, 768], P(('dp', 'seq'), None, 'mp')
- qv_bias_grad: float32 [2, 768], P(None, 'mp')
- proj_grad: float32 [768, 768], P(('dp', 'seq'), 'mp')
- proj_bias_grad: float32 [768], replicated
- first_gain_grad: float32 [768], replicated
- first_shift_grad: float32 [768], replicated
- up_grad: float32 [768, 3072], P(('dp', 'seq'), 'mp')
- up_bias_grad: float32 [3072], P('mp')
- down_grad: float32 [768, 3072], P(('dp', 'seq'), 'mp')
- down_bias_grad: float32 [768], replicated
- second_gain_grad: float32 [768], replicated
- second_shift_grad: float32 [768], replicated
Inputs may be any that keep to these rules, and one draw needn't show every extreme that they name: `segments`: segment numbers start at 0 and never fall along a sequence; among the 2 sequences of each index of dp one, drawn from the seed, is a single segment, and the others have 3 boundaries.
All inputs are finite; a program needn't handle non-finite values.
Results may differ from a plain program's by a relative error of at most 0.013.
The roundings to bfloat16 on the way count: a program that leaves them out, or rounds other values in their place, can miss the bound.
Values may be sent and summed in bfloat16 or wider, within the bound.
No kernel may reach another device: no remote copies, remote signals or barrier semaphores. Data moves between devices by JAX's collectives and lax.ppermute only.
A program may use at most 448 MiB of HBM per device.

v0:
```python
import jax
import jax.numpy as jnp
from jax import lax
from jax.sharding import PartitionSpec as P

HEAD = 64
MICRO = 2


EPS = 1e-06


def normalize(hidden):
    center = hidden - jnp.mean(hidden, -1, keepdims=True)
    spread = jnp.mean(center * center, -1, keepdims=True)
    return center * lax.rsqrt(spread + EPS)


def gelu_exact(values):
    return jax.nn.gelu(values, approximate=False)


def contract_last(left, right):
    return lax.dot_general(
        left, right, (((1,), (1,)), ((), ())), preferred_element_type=jnp.float32
    )


def contract_rows(left, right):
    return lax.dot_general(
        left, right, (((0,), (0,)), ((), ())), preferred_element_type=jnp.float32
    )


def head_total(partial_value):
    return lax.psum(partial_value, "mp")


def shards(
    hidden_in,
    segments,
    cotangent,
    qkv_weight,
    qv_bias,
    proj_weight,
    proj_bias,
    first_gain,
    first_shift,
    up_weight,
    up_bias,
    down_weight,
    down_bias,
    second_gain,
    second_shift,
):
    batch_all, local_len, width = hidden_in.shape
    per_micro = batch_all // MICRO
    inner = qkv_weight.shape[2]
    heads_here = inner // HEAD
    scale = HEAD ** (-0.5)
    hidden_units = up_weight.shape[1]
    row_count = per_micro * local_len
    share = row_count // lax.axis_size("mp")
    share_start = lax.axis_index("mp") * share

    def take(rows):
        return lax.dynamic_slice_in_dim(rows, share_start, share, 0)

    acc_qkv = jnp.zeros((width, 3, inner), jnp.float32)
    acc_proj = jnp.zeros((width, inner), jnp.float32)
    acc_up = jnp.zeros((width, hidden_units), jnp.float32)
    acc_down = jnp.zeros((width, hidden_units), jnp.float32)
    acc_qvbias = jnp.zeros((2, inner), jnp.float32)
    acc_upbias = jnp.zeros((hidden_units,), jnp.float32)
    acc_pbias = jnp.zeros((width,), jnp.float32)
    acc_dbias = jnp.zeros((width,), jnp.float32)
    acc_gain1 = jnp.zeros((width,), jnp.float32)
    acc_shift1 = jnp.zeros((width,), jnp.float32)
    acc_gain2 = jnp.zeros((width,), jnp.float32)
    acc_shift2 = jnp.zeros((width,), jnp.float32)
    out_blocks = []
    grad_blocks = []
    for micro_step in range(MICRO):
        lower = micro_step * per_micro
        upper = lower + per_micro
        tokens_low = hidden_in[lower:upper].reshape(-1, width)
        seg_local = segments[lower:upper]
        cot_rows = cotangent[lower:upper].reshape(-1, width).astype(jnp.float32)
        full_qkv, full_proj, full_up, full_down = (
            lax.all_gather(qkv_weight, ("dp", "seq"), axis=0, tiled=True),
            lax.all_gather(proj_weight, ("dp", "seq"), axis=0, tiled=True),
            lax.all_gather(up_weight, ("dp", "seq"), axis=0, tiled=True),
            lax.all_gather(down_weight, ("dp", "seq"), axis=0, tiled=True),
        )
        qkv_lin = jnp.einsum(
            "rd,dce->cre", tokens_low, full_qkv, preferred_element_type=jnp.float32
        )
        bias_rows = jnp.stack([qv_bias[0], jnp.zeros((inner,), jnp.float32), qv_bias[1]])
        qkv_low = (qkv_lin + bias_rows[:, None, :]).astype(jnp.bfloat16)
        queries = qkv_low[0].reshape(per_micro, local_len, heads_here, HEAD)
        keys_all, values_all, seg_all = (
            lax.all_gather(
                qkv_low[1].reshape(per_micro, local_len, inner), "seq", axis=1, tiled=True
            ),
            lax.all_gather(
                qkv_low[2].reshape(per_micro, local_len, inner), "seq", axis=1, tiled=True
            ),
            lax.all_gather(seg_local.astype(jnp.bfloat16), "seq", axis=1, tiled=True),
        )
        keys_heads = keys_all.reshape(per_micro, -1, heads_here, HEAD)
        values_heads = values_all.reshape(per_micro, -1, heads_here, HEAD)
        scores = (
            jnp.einsum("sqhd,skhd->shqk", queries, keys_heads, preferred_element_type=jnp.float32)
            * scale
        )
        allowed = (
            seg_local.astype(jnp.float32)[:, None, :, None]
            == seg_all.astype(jnp.float32)[:, None, None, :]
        )
        scores = jnp.where(allowed, scores, -1e30)
        top = jnp.max(scores, -1, keepdims=True)
        expo = jnp.exp(scores - top)
        probs = expo / jnp.sum(expo, -1, keepdims=True)
        probs_low = probs.astype(jnp.bfloat16)
        context = jnp.einsum(
            "shqk,skhd->sqhd", probs_low, values_heads, preferred_element_type=jnp.float32
        )
        context_low = context.reshape(-1, inner).astype(jnp.bfloat16)
        attn_partial = contract_last(context_low, full_proj)
        first_in = tokens_low.astype(jnp.float32) + head_total(attn_partial) + proj_bias
        unit_one, first_back = jax.vjp(normalize, first_in)
        normed = unit_one * first_gain + first_shift
        normed_low = normed.astype(jnp.bfloat16)
        pre_act = jnp.dot(normed_low, full_up, preferred_element_type=jnp.float32) + up_bias
        act_low = gelu_exact(pre_act).astype(jnp.bfloat16)
        down_partial = contract_last(act_low, full_down)
        back_qkv, back_proj, back_up, back_down = (
            lax.all_gather(qkv_weight, ("dp", "seq"), axis=0, tiled=True),
            lax.all_gather(proj_weight, ("dp", "seq"), axis=0, tiled=True),
            lax.all_gather(up_weight, ("dp", "seq"), axis=0, tiled=True),
            lax.all_gather(down_weight, ("dp", "seq"), axis=0, tiled=True),
        )
        second_in = normed + head_total(down_partial) + down_bias
        unit_two, second_back = jax.vjp(normalize, second_in)
        result = unit_two * second_gain + second_shift
        grad_second = second_back(cot_rows * second_gain)[0]
        acc_gain2 = acc_gain2 + jnp.sum(take(cot_rows * unit_two), 0)
        acc_shift2 = acc_shift2 + jnp.sum(take(cot_rows), 0)
        acc_dbias = acc_dbias + jnp.sum(take(grad_second), 0)
        out_low = result.astype(jnp.bfloat16)
        down_low = grad_second.astype(jnp.bfloat16)
        out_blocks.append(out_low.reshape(per_micro, local_len, width))
        acc_down = acc_down + contract_rows(down_low, act_low)
        grad_act = jnp.dot(down_low, back_down, preferred_element_type=jnp.float32)
        gelu_back = jax.vjp(gelu_exact, pre_act)[1]
        pre_low = gelu_back(grad_act)[0].astype(jnp.bfloat16)
        acc_upbias = acc_upbias + jnp.sum(pre_low.astype(jnp.float32), 0)
        acc_up = acc_up + contract_rows(normed_low, pre_low)
        normed_partial = contract_last(pre_low, back_up)
        grad_normed = grad_second + head_total(normed_partial)
        grad_first = first_back(grad_normed * first_gain)[0]
        acc_gain1 = acc_gain1 + jnp.sum(take(grad_normed * unit_one), 0)
        acc_shift1 = acc_shift1 + jnp.sum(take(grad_normed), 0)
        acc_pbias = acc_pbias + jnp.sum(take(grad_first), 0)
        attn_low = grad_first.astype(jnp.bfloat16)
        acc_proj = acc_proj + contract_rows(attn_low, context_low)
        grad_context = jnp.dot(attn_low, back_proj, preferred_element_type=jnp.float32).astype(
            jnp.bfloat16
        )
        grad_context = grad_context.reshape(per_micro, local_len, heads_here, HEAD)
        grad_values = jnp.einsum(
            "shqk,sqhd->skhd", probs_low, grad_context, preferred_element_type=jnp.float32
        )
        grad_probs = jnp.einsum(
            "sqhd,skhd->shqk", grad_context, values_heads, preferred_element_type=jnp.float32
        )
        delta = jnp.sum(probs * grad_probs, -1, keepdims=True)
        grad_scores = (probs * (grad_probs - delta)).astype(jnp.bfloat16) * scale
        grad_queries = jnp.einsum(
            "shqk,skhd->sqhd", grad_scores, keys_heads, preferred_element_type=jnp.float32
        )
        grad_keys = jnp.einsum(
            "shqk,sqhd->skhd", grad_scores, queries, preferred_element_type=jnp.float32
        )
        key_part, value_part = (
            lax.psum_scatter(
                grad_keys.reshape(per_micro, -1, inner), "seq", scatter_dimension=1, tiled=True
            ),
            lax.psum_scatter(
                grad_values.reshape(per_micro, -1, inner), "seq", scatter_dimension=1, tiled=True
            ),
        )
        grad_qkv = jnp.stack(
            [
                grad_queries.reshape(-1, inner),
                key_part.reshape(-1, inner),
                value_part.reshape(-1, inner),
            ]
        ).astype(jnp.bfloat16)
        grad_sums = jnp.sum(grad_qkv.astype(jnp.float32), 1)
        acc_qvbias = acc_qvbias + jnp.stack([grad_sums[0], grad_sums[2]])
        acc_qkv = acc_qkv + jnp.einsum(
            "rd,cre->dce", tokens_low, grad_qkv, preferred_element_type=jnp.float32
        )
        input_part = jnp.einsum(
            "cre,dce->rd", grad_qkv, back_qkv, preferred_element_type=jnp.float32
        )
        input_full = grad_first + head_total(input_part)
        grad_blocks.append(input_full.reshape(per_micro, local_len, width))
    qkv_owned, proj_owned, up_owned, down_owned = (
        lax.psum_scatter(acc_qkv, ("dp", "seq"), scatter_dimension=0, tiled=True),
        lax.psum_scatter(acc_proj, ("dp", "seq"), scatter_dimension=0, tiled=True),
        lax.psum_scatter(acc_up, ("dp", "seq"), scatter_dimension=0, tiled=True),
        lax.psum_scatter(acc_down, ("dp", "seq"), scatter_dimension=0, tiled=True),
    )
    split_sums = lax.psum((acc_qvbias, acc_upbias), ("dp", "seq"))
    norm_sums = lax.psum(
        (acc_pbias, acc_gain1, acc_shift1, acc_dbias, acc_gain2, acc_shift2), ("dp", "seq", "mp")
    )
    layer_out = jnp.concatenate(out_blocks, 0)
    input_grad = jnp.concatenate(grad_blocks, 0)
    return (
        layer_out,
        input_grad,
        qkv_owned,
        split_sums[0],
        proj_owned,
        norm_sums[0],
        norm_sums[1],
        norm_sums[2],
        up_owned,
        split_sums[1],
        down_owned,
        norm_sums[3],
        norm_sums[4],
        norm_sums[5],
    )


def solution(mesh):
    in_specs = (
        P("dp", "seq", None),
        P("dp", "seq"),
        P("dp", "seq", None),
        P(("dp", "seq"), None, "mp"),
        P(None, "mp"),
        P(("dp", "seq"), "mp"),
        P(),
        P(),
        P(),
        P(("dp", "seq"), "mp"),
        P("mp"),
        P(("dp", "seq"), "mp"),
        P(),
        P(),
        P(),
    )
    out_specs = (
        P("dp", "seq", None),
        P("dp", "seq", None),
        P(("dp", "seq"), None, "mp"),
        P(None, "mp"),
        P(("dp", "seq"), "mp"),
        P(),
        P(),
        P(),
        P(("dp", "seq"), "mp"),
        P("mp"),
        P(("dp", "seq"), "mp"),
        P(),
        P(),
        P(),
    )
    return jax.shard_map(shards, mesh=mesh, in_specs=in_specs, out_specs=out_specs, check_vma=False)
```

profile of v0, /device:TPU:0, one launch (start us, length us, event | category | flops | bytes accessed | tf_op | source)
XLA Modules:
  0.0 1326.8 jit_solution(4857223675715046567)
XLA Ops:
  9.9 41.6 %all_gather.20 = bf16[768,3,192]{2,1,0:T(4,128)(2,1)S(1)} all-gather(bf16[96,3,192]{2,1,0:T(4,128)(2,1)S(1)} %copy.33), channel_id=1, replica_groups=mesh['dp'=2,'seq'=4,'mp'=4] {'dp','seq'}, dimensions={0}, use_global_device_ids=true | all-gather | bytes 995328 | tf_op jit(solution)/shard_map/all_gather | solution.py:90
  61.9 13.4 %all_gather.44 = bf16[1,4096]{1,0:T(2,128)(2,1)S(1)} all-gather(bf16[1,1024]{1,0:T(2,128)(2,1)S(1)} %get-tuple-element.117), channel_id=1, replica_groups=mesh['dp'=2,'seq'=4,'mp'=4] {'seq'}, dimensions={1}, use_global_device_ids=true | all-gather | bytes 10240 | tf_op jit(solution)/shard_map/all_gather | solution.py:108
  75.3 13.2 all_gather.50
  88.5 33.0 %all_gather.46 = bf16[768,192]{1,0:T(8,128)(2,1)S(1)} all-gather(bf16[96,192]{1,0:T(8,128)(2,1)S(1)} %copy-done.44), channel_id=1, replica_groups=mesh['dp'=2,'seq'=4,'mp'=4] {'dp','seq'}, dimensions={0}, use_global_device_ids=true | all-gather | bytes 331776 | tf_op jit(solution)/shard_map/all_gather | solution.py:91
  131.1 24.5 %fusion.174 = (f32[3,1024]{1,0:T(4,128)S(1)}, f32[3,1024,4096]{2,1,0:T(8,128)}) fusion(pred[1024,4096]{1,0:T(8,128)(4,1)} %broadcast_compare_fusion.1, bf16[1024,3,64]{0,2,1:T(8,128)(2,1)S(1)} %bitcast.172, bf16[4096,3,64]{0,2,1:T(8,128)(2,1)} %bitcast.186), kind=kOutput, calls=%fused_computation.241 | convolution fusion | flops 1660948480 | bytes 56504320 | tf_op jit(solution)/shard_map/sub | solution.py:122
  155.6 18.3 %fusion.99 = bf16[3,64,1024]{2,1,0:T(8,128)(2,1)S(1)} fusion(bf16[4096,3,64]{0,2,1:T(8,128)(2,1)} %bitcast.159, f32[3,1024,4096]{2,1,0:T(8,128)} %get-tuple-element.137, f32[3,1024]{1,0:T(4,128)S(1)} %get-tuple-element.136), kind=kOutput, calls=%fused_computation.144 | convolution fusion | flops 1635975168 | bytes 52310016 | tf_op jit(solution)/shard_map/shqk,skhd->sqhd/dot_general | solution.py:125
  177.0 24.4 %fusion.173 = (f32[3,1024]{1,0:T(4,128)S(1)}, f32[3,1024,4096]{2,1,0:T(8,128)}) fusion(pred[1024,4096]{1,0:T(8,128)(4,1)} %broadcast_compare_fusion, bf16[1024,3,64]{0,2,1:T(8,128)(2,1)S(1)} %bitcast.174, bf16[4096,3,64]{0,2,1:T(8,128)(2,1)} %bitcast.188), kind=kOutput, calls=%fused_computation.240 | convolution fusion | flops 1660948480 | bytes 56504320 | tf_op jit(solution)/shard_map/sub | solution.py:122
  210.3 18.5 %fusion.102 = bf16[3,64,1024]{2,1,0:T(8,128)(2,1)S(1)} fusion(bf16[4096,3,64]{0,2,1:T(8,128)(2,1)} %bitcast.161, f32[3,1024,4096]{2,1,0:T(8,128)} %get-tuple-element.135, f32[3,1024]{1,0:T(4,128)S(1)} %get-tuple-element.134), kind=kOutput, calls=%fused_computation.145 | convolution fusion | flops 1635975168 | bytes 52310016 | tf_op jit(solution)/shard_map/shqk,skhd->sqhd/dot_general | solution.py:125
  233.2 117.6 %all-reduce.17.cloned.1.call-done = (f32[1024,768]{1,0:T(8,128)}, f32[1024,768]{1,0:T(8,128)}) async-done(((f32[1024,768]{1,0:T(8,128)}, f32[1024,768]{1,0:T(8,128)}), (f32[1024,768]{1,0:T(8,128)}, f32[1024,768]{1,0:T(8,128)})) %all-reduce.17.cloned.1.call-update) | async-done | bytes 6291472 | tf_op jit(solution)/shard_map/psum | solution.py:36
  365.9 16.4 %multiply_convert_fusion.3 = (bf16[1024,768]{1,0:T(8,128)(2,1)}, f32[1024,768]{1,0:T(8,128)}, bf16[1024,768]{1,0:T(8,128)(2,1)}, f32[1024,768]{1,0:T(8,128)}, f32[1024,768]{1,0:T(8,128)}) fusion(f32[768]{0:T(1024)S(1)} %copy-done.72, f32[1024,768]{1,0:T(8,128)S(1)} %fusion.132, bf16[768,768]{1,0:T(8,128)(2,1)S(1)} %copy-done.68, ...), kind=kOutput, calls=%fused_computation.90 | convolution fusion | flops 1314127872 | bytes 20063232 | tf_op jit(solution)/shard_map/dot_general | solution.py:134
  390.5 120.1 %all-reduce.15.cloned.1.call-done = (f32[1024,768]{1,0:T(8,128)}, f32[1024,768]{1,0:T(8,128)}) async-done(((f32[1024,768]{1,0:T(8,128)}, f32[1024,768]{1,0:T(8,128)}), (f32[1024,768]{1,0:T(8,128)}, f32[1024,768]{1,0:T(8,128)})) %all-reduce.15.cloned.1.call-update) | async-done | bytes 6291472 | tf_op jit(solution)/shard_map/psum | solution.py:36
  546.0 120.1 %all-reduce.13.cloned.1.call-done = (f32[1024,768]{1,0:T(8,128)}, f32[1024,768]{1,0:T(8,128)}) async-done(((f32[1024,768]{1,0:T(8,128)}, f32[1024,768]{1,0:T(8,128)}), (f32[1024,768]{1,0:T(8,128)}, f32[1024,768]{1,0:T(8,128)})) %all-reduce.13.cloned.1.call-update) | async-done | bytes 6291472 | tf_op jit(solution)/shard_map/psum | solution.py:36
  681.4 18.8 %fusion.50 = f32[3,64,4096]{2,1,0:T(8,128)} fusion(bf16[1024,3,64]{0,2,1:T(8,128)(2,1)S(1)} %bitcast.163, f32[3,1024,4096]{2,1,0:T(8,128)} %get-tuple-element.137, f32[3,1024]{1,0:T(4,128)S(1)} %copy-done.85), kind=kOutput, calls=%fused_computation.40 | convolution fusion | flops 1635778560 | bytes 53882880 | tf_op jit(solution)/shard_map/shqk,sqhd->skhd/dot_general | solution.py:171
  704.9 19.4 %fusion.46 = f32[3,64,4096]{2,1,0:T(8,128)} fusion(bf16[1024,3,64]{0,2,1:T(8,128)(2,1)S(1)} %bitcast.165, f32[3,1024,4096]{2,1,0:T(8,128)} %get-tuple-element.135, f32[3,1024]{1,0:T(4,128)S(1)} %copy-done.88), kind=kOutput, calls=%fused_computation.36 | convolution fusion | flops 1635778560 | bytes 53882880 | tf_op jit(solution)/shard_map/shqk,sqhd->skhd/dot_general | solution.py:171
  725.8 19.6 %fusion.182 = f32[3,1024,4096]{2,1,0:T(8,128)} fusion(bf16[1024,3,64]{0,2,1:T(8,128)(2,1)S(1)} %bitcast.166, bf16[4096,3,64]{0,2,1:T(8,128)(2,1)S(1)} %bitcast.162), kind=kOutput, calls=%fused_computation.249 | convolution fusion | flops 1610612736 | bytes 52297728 | tf_op jit(solution)/shard_map/sqhd,skhd->shqk/dot_general | solution.py:174
  745.3 63.9 %fusion.18 = f32[3,64,4096]{2,1,0:T(8,128)} fusion(bf16[1024,3,64]{0,2,1:T(8,128)(2,1)S(1)} %bitcast.175, f32[3,1024,4096]{2,1,0:T(8,128)} %fusion.182, f32[3,1024,4096]{2,1,0:T(8,128)} %get-tuple-element.135, f32[3,1024]{1,0:T(4,128)S(1)} %copy-done.88), kind=kOutput, calls=%fused_computation.24 | convolution fusion | flops 1736449024 | bytes 104214528 | tf_op jit(solution)/shard_map/shqk,sqhd->skhd/dot_general | solution.py:182
  810.7 19.9 %fusion.180 = f32[3,1024,4096]{2,1,0:T(8,128)} fusion(bf16[1024,3,64]{0,2,1:T(8,128)(2,1)S(1)} %bitcast.164, bf16[4096,3,64]{0,2,1:T(8,128)(2,1)S(1)} %bitcast.160), kind=kOutput, calls=%fused_computation.247 | convolution fusion | flops 1610612736 | bytes 52297728 | tf_op jit(solution)/shard_map/sqhd,skhd->shqk/dot_general | solution.py:174
  830.6 64.0 %fusion.30 = f32[3,64,4096]{2,1,0:T(8,128)} fusion(bf16[1024,3,64]{0,2,1:T(8,128)(2,1)S(1)} %bitcast.173, f32[3,1024,4096]{2,1,0:T(8,128)} %fusion.180, f32[3,1024,4096]{2,1,0:T(8,128)} %get-tuple-element.137, f32[3,1024]{1,0:T(4,128)S(1)} %copy-done.86), kind=kOutput, calls=%fused_computation.28 | convolution fusion | flops 1736449024 | bytes 104214528 | tf_op jit(solution)/shard_map/shqk,sqhd->skhd/dot_general | solution.py:182
  894.7 62.5 %fusion.94 = bf16[3,64,1024]{2,1,0:T(8,128)(2,1)S(1)} fusion(bf16[4096,3,64]{0,2,1:T(8,128)(2,1)} %bitcast.189, f32[3,1024,4096]{2,1,0:T(8,128)} %fusion.182, f32[3,1024,4096]{2,1,0:T(8,128)} %get-tuple-element.135, f32[3,1024]{1,0:T(4,128)S(1)} %copy-done.88), kind=kOutput, calls=%fused_computation.141 | convolution fusion | flops 1736645632 | bytes 102641664 | tf_op jit(solution)/shard_map/shqk,skhd->sqhd/dot_general | solution.py:179
  957.2 62.1 %fusion.89 = bf16[3,64,1024]{2,1,0:T(8,128)(2,1)S(1)} fusion(bf16[4096,3,64]{0,2,1:T(8,128)(2,1)S(1)} %bitcast.187, f32[3,1024,4096]{2,1,0:T(8,128)} %fusion.180, f32[3,1024,4096]{2,1,0:T(8,128)} %get-tuple-element.137, f32[3,1024]{1,0:T(4,128)S(1)} %copy-done.86), kind=kOutput, calls=%fused_computation.140 | convolution fusion | flops 1736645632 | bytes 102641664 | tf_op jit(solution)/shard_map/shqk,skhd->sqhd/dot_general | solution.py:179
  1074.8 42.1 %all-reduce = (f32[768]{0:T(1024)}, f32[768]{0:T(1024)}, f32[768]{0:T(1024)}, f32[768]{0:T(1024)}, f32[768]{0:T(1024)}, /*index=5*/f32[768]{0:T(1024)}) all-reduce(f32[768]{0:T(1024)S(1)} %add.286, f32[768]{0:T(1024)} %add.287, f32[768]{0:T(1024)} %add.288, f32[768]{0:T(1024)} %add.292, ...), channel_id=1, replica_groups=mesh['dp'=2,'seq'=4,'mp'=4] {'dp','seq','mp'}, use_global_device_ids=true, to_apply=%region_41.42 | all-reduce | flops 4608 | bytes 36864 | tf_op jit(solution)/shard_map/psum | solution.py:217
  1119.8 22.6 %all-reduce.1 = (f32[2,192]{1,0:T(2,128)}, f32[768]{0:T(1024)}) all-reduce(f32[2,192]{1,0:T(2,128)S(1)} %maximum_add_fusion, f32[768]{0:T(1024)S(1)} %add.290), channel_id=1, replica_groups=mesh['dp'=2,'seq'=4,'mp'=4] {'dp','seq'}, use_global_device_ids=true, to_apply=%region_37.38 | all-reduce | flops 1152 | bytes 9216 | tf_op jit(solution)/shard_map/psum | solution.py:216
  1174.4 72.4 %reduce-scatter.23.cloned.1.call-done = f32[96,768]{1,0:T(8,128)} async-done(((f32[768,768]{1,0:T(8,128)}), f32[96,768]{1,0:T(8,128)}) %reduce-scatter.23.cloned.1.call-update) | async-done | bytes 294928 | tf_op jit(solution)/shard_map/reduce_scatter | solution.py:214
  1246.8 72.4 %reduce-scatter.21.cloned.1.call-done = f32[96,768]{1,0:T(8,128)} async-done(((f32[768,768]{1,0:T(8,128)}), f32[96,768]{1,0:T(8,128)}) %reduce-scatter.21.cloned.1.call-update) | async-done | bytes 294928 | tf_op jit(solution)/shard_map/reduce_scatter | solution.py:213
  (321 shorter events, 208.8 us)
Async XLA Ops:
  8.0 123.1 %all-gather.9.cloned.1.call-start = ((), (), s32[]{:S(2)}) async-start(), calls=%async_computation.9 | async-start | bytes 1966080 | tf_op jit(solution)/shard_map/all_gather | solution.py:102
  56.0 99.6 %all-gather.7.cloned.1.call-start = ((), (), s32[]{:S(2)}) async-start(), calls=%async_computation.8 | async-start | bytes 1966080 | tf_op jit(solution)/shard_map/all_gather | solution.py:105
  56.8 120.2 %all-gather.17.cloned.1.call-start = ((), (), s32[]{:S(2)}) async-start(), calls=%async_computation.13 | async-start | bytes 1966080 | tf_op jit(solution)/shard_map/all_gather | solution.py:102
  60.2 28.3 %copy-start.44 = (bf16[96,192]{1,0:T(8,128)(2,1)S(1)}, bf16[96,192]{1,0:T(8,128)(2,1)}, u32[]{:S(2)}) copy-start(bf16[96,192]{1,0:T(8,128)(2,1)} %param.20) | copy-start | bytes 110596
  61.2 115.8 %copy-start.39 = (bf16[1,1024,192]{1,2,0:T(8,128)(2,1)}, bf16[1,1024,192]{1,2,0:T(8,128)(2,1)S(1)}, u32[]{:S(2)}) copy-start(bf16[1,1024,192]{1,2,0:T(8,128)(2,1)S(1)} %get-tuple-element.112) | copy-start | bytes 1179652
  61.2 149.1 %all-gather.15.cloned.1.call-start = ((), (), s32[]{:S(2)}) async-start(), calls=%async_computation.12 | async-start | bytes 1966080 | tf_op jit(solution)/shard_map/all_gather | solution.py:105
  61.8 289.0 %all-reduce.17.cloned.1.call-start = ((), (), s32[]{:S(2)}) async-start(), calls=%async_computation.25 | async-start | bytes 12582912 | tf_op jit(solution)/shard_map/psum | solution.py:36
  231.9 118.8 %copy-start.64 = (f32[768]{0:T(1024)S(1)}, f32[768]{0:T(1024)}, u32[]{:S(2)}) copy-start(f32[768]{0:T(1024)} %param.21) | copy-start | bytes 9220
  231.9 128.5 %all-gather.11.cloned.1.call-start = ((), (), s32[]{:S(2)}) async-start(), calls=%async_computation.10 | async-start | bytes 1327104 | tf_op jit(solution)/shard_map/all_gather | solution.py:92
  232.5 149.8 %all-gather.13.cloned.1.call-start = ((), (), s32[]{:S(2)}) async-start(), calls=%async_computation.11 | async-start | bytes 1327104 | tf_op jit(solution)/shard_map/all_gather | solution.py:93
  233.1 277.5 %all-reduce.15.cloned.1.call-start = ((), (), s32[]{:S(2)}) async-start(), calls=%async_computation.24 | async-start | bytes 12582912 | tf_op jit(solution)/shard_map/psum | solution.py:36
  390.5 275.6 %all-reduce.13.cloned.1.call-start = ((), (), s32[]{:S(2)}) async-start(), calls=%async_computation.23 | async-start | bytes 12582912 | tf_op jit(solution)/shard_map/psum | solution.py:36
  545.9 473.5 %reduce-scatter.13.cloned.1.call-start = ((), (), s32[]{:S(2)}) async-start(), calls=%async_computation.15 | async-start | bytes 3932160 | tf_op jit(solution)/shard_map/reduce_scatter | solution.py:189
  700.2 320.6 %reduce-scatter.17.cloned.1.call-start = ((), (), s32[]{:S(2)}) async-start(), calls=%async_computation.17 | async-start | bytes 3932160 | tf_op jit(solution)/shard_map/reduce_scatter | solution.py:189
  724.4 297.6 %reduce-scatter.15.cloned.1.call-start = ((), (), s32[]{:S(2)}) async-start(), calls=%async_computation.16 | async-start | bytes 3932160 | tf_op jit(solution)/shard_map/reduce_scatter | solution.py:186
  809.2 217.3 %reduce-scatter.11.cloned.1.call-start = ((), (), s32[]{:S(2)}) async-start(), calls=%async_computation.14 | async-start | bytes 3932160 | tf_op jit(solution)/shard_map/reduce_scatter | solution.py:186
  894.6 62.6 %copy-start.67 = (bf16[1,4096,192]{1,2,0:T(8,128)(2,1)S(1)}, bf16[1,4096,192]{1,2,0:T(8,128)(2,1)}, u32[]{:S(2)}) copy-start(bf16[1,4096,192]{1,2,0:T(8,128)(2,1)} %all-gather.9.cloned.1.call-done) | copy-start | bytes 4718596
  894.6 257.8 %all-reduce.11.cloned.1.call-start = ((), (), s32[]{:S(2)}) async-start(), calls=%async_computation.22 | async-start | bytes 12582912 | tf_op jit(solution)/shard_map/psum | solution.py:36
  957.2 66.2 %copy-start.41 = (bf16[3,64,1024]{2,1,0:T(8,128)(2,1)}, bf16[3,64,1024]{2,1,0:T(8,128)(2,1)S(1)}, u32[]{:S(2)}) copy-start(bf16[3,64,1024]{2,1,0:T(8,128)(2,1)S(1)} %fusion.94) | copy-start | bytes 1179652
  1030.9 129.8 %reduce-scatter.25.cloned.1.call-start = ((), (), s32[]{:S(2)}) async-start(), calls=%async_computation.21 | async-start | bytes 2211840
  1040.6 133.8 %reduce-scatter.19.cloned.1.call-start = ((), (), s32[]{:S(2)}) async-start(), calls=%async_computation.18 | async-start | bytes 884736 | tf_op jit(solution)/shard_map/reduce_scatter | solution.py:212
  1044.3 202.5 %reduce-scatter.23.cloned.1.call-start = ((), (), s32[]{:S(2)}) async-start(), calls=%async_computation.20 | async-start | bytes 2654208 | tf_op jit(solution)/shard_map/reduce_scatter | solution.py:214
  1051.3 267.8 %reduce-scatter.21.cloned.1.call-start = ((), (), s32[]{:S(2)}) async-start(), calls=%async_computation.19 | async-start | bytes 2654208 | tf_op jit(solution)/shard_map/reduce_scatter | solution.py:213
  1070.7 81.7 %copy-start.50 = (f32[1024]{0:T(1024)S(1)}, f32[1024]{0:T(1024)}, u32[]{:S(2)}) copy-start(f32[1024]{0:T(1024)} %copy-done.49) | copy-start | bytes 12292
  (83 other events, 396.5 us)
Sparse Core Ops, SparseCore 0:
  56.1 38.9 all-gather.8
  96.7 37.8 all-gather.6
  136.8 36.0 all-gather.16
  174.3 35.9 all-gather.14
  232.1 118.6 all-reduce.16
  390.6 119.9 all-reduce.14
  546.1 119.9 all-reduce.12
  700.4 60.4 reduce-scatter.12
  763.7 60.2 reduce-scatter.16
  826.2 60.2 reduce-scatter.14
  894.7 60.4 reduce-scatter.10
  1031.1 121.3 all-reduce.10
Sparse Core Ops, SparseCore 1:
  234.5 40.2 all-gather.10
  276.7 39.8 all-gather.12
  1040.7 67.3 reduce-scatter.24
  1112.3 62.0 reduce-scatter.18
  1178.4 68.3 reduce-scatter.22
  1250.8 68.2 reduce-scatter.20
where the time goes:
time: 1330 us
  waiting for transfers between devices  536 us (40%)
  matrix products  497 us (37%)
  blocking collectives  166 us (12%)
  other arithmetic  75.2 us (6%)
  local copies, waits for them, and re-layouts  35.3 us (3%)
  between operations  17 us (1%)
    psum x4, waiting for transfers between devices, head_total(): return lax.psum(partial_value, 'mp')  368 us
    dot_general x2, matrix products, shards(): jnp.einsum('shqk,sqhd->skhd', grad_scores, queries, preferred_element_typ...  128 us
    dot_general x2, matrix products, shards(): jnp.einsum('shqk,skhd->sqhd', grad_scores, keys_heads, preferred_element_...  125 us
    reduce_scatter x1, waiting for transfers between devices, shards(): lax.psum_scatter(acc_down, ('dp', 'seq'), scatter_dimension=0, tiled=True)  72.4 us
    reduce_scatter x1, waiting for transfers between devices, shards(): lax.psum_scatter(acc_up, ('dp', 'seq'), scatter_dimension=0, tiled=True)  72.4 us
    sub x2, matrix products, shards(): expo = jnp.exp(scores - top)  49 us
    psum x1, blocking collectives, shards(): lax.psum((acc_pbias, acc_gain1, acc_shift1, acc_dbias, acc_gain2, acc_shi...  42.1 us
    all_gather x1, blocking collectives, shards(): lax.all_gather(qkv_weight, ('dp', 'seq'), axis=0, tiled=True)  41.6 us
  transfers between devices with their start and end apart: 18, of which 8 were waited for; matrix products, arithmetic and copies ran while one was open for 37% of the time, Pallas kernels for 0%

commit v1 on v0

v1 whole, which is shorter than its diff:
```python
import functools

import jax
import jax.numpy as jnp
from jax import lax
from jax.experimental import pallas as pl
from jax.experimental.pallas import tpu as pltpu
from jax.sharding import PartitionSpec as P

HEAD = 64
EPS = 1e-06
SCALE = HEAD**-0.5
CEXP = 1.4426950408889634 * SCALE
QB = 512
KB = 512
NT = (((1,), (1,)), ((), ()))
NN = (((1,), (0,)), ((), ()))
TN = (((0,), (0,)), ((), ()))
VMEM = pl.BlockSpec(memory_space=pltpu.VMEM)
SMEM = pl.BlockSpec(memory_space=pltpu.SMEM)
PARAMS = pltpu.CompilerParams(vmem_limit_bytes=48 * 2**20)
LOW = jnp.bfloat16
FLIP = (0, 2, 1, 3)


def dot(left, right, dims):
    return lax.dot_general(left, right, dims, preferred_element_type=jnp.float32)


def visit(bounds, qi, kj, work):
    qlo, qhi, klo, khi = bounds[0, qi], bounds[1, qi], bounds[2, kj], bounds[3, kj]
    overlap = (qlo <= khi) & (klo <= qhi)
    pure = (qlo == qhi) & (klo == khi) & (qlo == klo)
    pl.when(pure)(lambda: work(False))
    pl.when(overlap & jnp.logical_not(pure))(lambda: work(True))


def fwd_body(first, bounds, segq, segk, q, k, vt, *rest):
    if first:
        top, total, acc = rest
        top[...] = jnp.full(top.shape, -1e30, jnp.float32)
        total[...] = jnp.zeros(total.shape, jnp.float32)
        acc[...] = jnp.zeros(acc.shape, jnp.float32)
    else:
        top_in, total_in, acc_in, top, total, acc = rest
        top[...] = top_in[...]
        total[...] = total_in[...]
        acc[...] = acc_in[...]

    def qstep(qi, _):
        qs = pl.ds(pl.multiple_of(qi * QB, QB), QB)

        def kstep(kj, _):
            ks = pl.ds(pl.multiple_of(kj * KB, KB), KB)

            def work(masked):
                if masked:
                    bad = segk[ks, :] != segq[0:1, qs]
                for h in range(q.shape[1] // HEAD):
                    c = slice(h * HEAD, (h + 1) * HEAD)
                    s = dot(k[ks, c], q[qs, c], NT) * CEXP
                    if masked:
                        s = jnp.where(bad, -1e30, s)
                    old = top[h : h + 1, qs]
                    new = jnp.maximum(old, jnp.max(s, 0, keepdims=True))
                    p = jnp.exp2(s - new)
                    shrink = jnp.exp2(old - new)
                    top[h : h + 1, qs] = new
                    total[h : h + 1, qs] = total[h : h + 1, qs] * shrink + jnp.sum(p, 0, keepdims=True)
                    acc[c, qs] = acc[c, qs] * shrink + dot(vt[c, ks], p.astype(LOW), NN)

            visit(bounds, qi, kj, work)
            return 0

        lax.fori_loop(0, k.shape[0] // KB, kstep, 0)
        return 0

    lax.fori_loop(0, q.shape[0] // QB, qstep, 0)


def attend(bounds, segq, segk, q, k, vt, state):
    rows, inner = q.shape
    stats = jax.ShapeDtypeStruct((8, rows), jnp.float32)
    return pl.pallas_call(
        functools.partial(fwd_body, not state),
        out_shape=(stats, stats, jax.ShapeDtypeStruct((inner, rows), jnp.float32)),
        in_specs=[SMEM] + [VMEM] * (5 + len(state)),
        out_specs=(VMEM,) * 3,
        compiler_params=PARAMS,
    )(bounds, segq, segk, q, k, vt, *state)


def bwd_body(first, bounds, segq, segk, q, do, lse, delta, k, kt, v, *rest):
    if first:
        dq, dk, dv = rest
        dq[...] = jnp.zeros(dq.shape, jnp.float32)
    else:
        dq_in, dq, dk, dv = rest
        dq[...] = dq_in[...]
    dk[...] = jnp.zeros(dk.shape, jnp.float32)
    dv[...] = jnp.zeros(dv.shape, jnp.float32)

    def kstep(kj, _):
        ks = pl.ds(pl.multiple_of(kj * KB, KB), KB)

        def qstep(qi, _):
            qs = pl.ds(pl.multiple_of(qi * QB, QB), QB)

            def work(masked):
                if masked:
                    bad = segk[ks, :] != segq[0:1, qs]
                for h in range(q.shape[1] // HEAD):
                    c = slice(h * HEAD, (h + 1) * HEAD)
                    qh = q[qs, c]
                    dh = do[qs, c]
                    s = dot(k[ks, c], qh, NT) * CEXP - lse[h : h + 1, qs]
                    if masked:
                        s = jnp.where(bad, -1e30, s)
                    p = jnp.exp2(s)
                    dp = dot(v[ks, c], dh, NT)
                    ds = (p * (dp - delta[h : h + 1, qs])).astype(LOW)
                    dv[ks, c] += dot(p.astype(LOW), dh, NN)
                    dk[ks, c] += dot(ds, qh, NN)
                    dq[c, qs] += dot(kt[c, ks], ds, NN)

            visit(bounds, qi, kj, work)
            return 0

        lax.fori_loop(0, q.shape[0] // QB, qstep, 0)
        return 0

    lax.fori_loop(0, k.shape[0] // KB, kstep, 0)


def attend_back(bounds, segq, segk, q, do, lse, delta, k, kt, v, state):
    rows, inner = q.shape
    by_key = jax.ShapeDtypeStruct(k.shape, jnp.float32)
    return pl.pallas_call(
        functools.partial(bwd_body, not state),
        out_shape=(jax.ShapeDtypeStruct((inner, rows), jnp.float32), by_key, by_key),
        in_specs=[SMEM] + [VMEM] * (9 + len(state)),
        out_specs=(VMEM,) * 3,
        compiler_params=PARAMS,
    )(bounds, segq, segk, q, do, lse, delta, k, kt, v, *state)


def normalize(hidden):
    center = hidden - jnp.mean(hidden, -1, keepdims=True)
    spread = jnp.mean(center * center, -1, keepdims=True)
    return center * lax.rsqrt(spread + EPS)


def flip(value, axis, bit):
    size = lax.axis_size(axis)
    return lax.ppermute(value, axis, [(i, i ^ bit) for i in range(size)])


def onward(value):
    size = lax.axis_size("seq")
    return lax.ppermute(value, "seq", [(i, (i + 1) % size) for i in range(size)])


def low_sum(left, right):
    return (left.astype(jnp.float32) + right.astype(jnp.float32)).astype(LOW)


def shards(
    hidden_in,
    segments,
    cotangent,
    qkv_weight,
    qv_bias,
    proj_weight,
    proj_bias,
    first_gain,
    first_shift,
    up_weight,
    up_bias,
    down_weight,
    down_bias,
    second_gain,
    second_shift,
):
    batch, local_len, width = hidden_in.shape
    inner = qkv_weight.shape[2]
    heads = inner // HEAD
    units = up_weight.shape[1]
    n_dp, n_seq, n_mp = lax.axis_size("dp"), lax.axis_size("seq"), lax.axis_size("mp")
    assert n_mp == 4
    d_at, s_at, m_at = lax.axis_index("dp"), lax.axis_index("seq"), lax.axis_index("mp")
    chunk_at = (m_at % 2) * 2 + m_at // 2
    share = local_len // n_mp
    own_rows = batch * share
    shard_rows = qkv_weight.shape[0]
    halves = n_dp == 2

    def place(pieces, positions):
        rows = pieces[0].shape[0]
        whole = jnp.zeros((rows * len(pieces),) + pieces[0].shape[1:], pieces[0].dtype)
        for piece, position in zip(pieces, positions):
            whole = lax.dynamic_update_slice_in_dim(whole, piece, position * rows, 0)
        return whole

    def relative(rows):
        return jnp.concatenate(
            [lax.dynamic_slice_in_dim(rows, (chunk_at ^ i) * share, share, 0) for i in range(4)], 0
        )

    def own(rows):
        return lax.dynamic_slice_in_dim(rows, chunk_at * share, share, 1).reshape(own_rows, -1)

    def swapped(rows):
        if not halves:
            return rows
        first, second = jnp.split(rows, 2, -1)
        return jnp.where(d_at == 1, jnp.concatenate([second, first], -1), rows)

    def share_over_mp(piece):
        pair = jnp.concatenate([piece, flip(piece, "mp", 2)], 0)
        return jnp.concatenate([pair, flip(pair, "mp", 1)], 0)

    def sum_over_mp(rows):
        half = rows.shape[0] // 2
        pair = low_sum(rows[:half], flip(rows[half:], "mp", 1))
        quarter = half // 2
        return pair[:quarter].astype(jnp.float32) + flip(pair[quarter:], "mp", 2).astype(jnp.float32)

    flat_qkv = qkv_weight.reshape(shard_rows, 3 * inner)
    if halves:
        pieces, positions = [flat_qkv], [d_at * n_seq + s_at]
        for dy in range(2):
            for dz in range(n_seq):
                if dy or dz:
                    pairs = [
                        (y * n_seq + z, (y ^ dy) * n_seq + (z + dz) % n_seq)
                        for y in range(2)
                        for z in range(n_seq)
                    ]
                    pieces.append(lax.ppermute(flat_qkv, ("dp", "seq"), pairs))
                    positions.append((d_at ^ dy) * n_seq + (s_at - dz) % n_seq)
        full_qkv = place(pieces, positions)
    else:
        full_qkv = lax.all_gather(flat_qkv, ("dp", "seq"), axis=0, tiled=True)
    weight_q, weight_k, weight_v = (full_qkv[:, i * inner : (i + 1) * inner] for i in range(3))

    seg_now = segments.astype(jnp.float32)
    seg_whole = [lax.all_gather(seg_now.astype(LOW), "seq", axis=0, tiled=False)]
    hidden_blocks = [[relative(hidden_in[b]) for b in range(batch)]]
    seg_blocks = [[relative(seg_now[b]) for b in range(batch)]]
    travel = [hidden_blocks[0][b][:share] for b in range(batch)]
    for t in range(1, n_seq):
        travel = [onward(piece) for piece in travel]
        hidden_blocks.append([share_over_mp(piece) for piece in travel])
        source = (s_at - t) % n_seq
        seg_there = lax.dynamic_index_in_dim(seg_whole[0], source, 0, keepdims=False)
        seg_blocks.append([relative(seg_there[b].astype(jnp.float32)) for b in range(batch)])

    def limits(queries, keys):
        parts_q, parts_k = queries.reshape(-1, QB), keys.reshape(-1, KB)
        return jnp.stack(
            [jnp.min(parts_q, 1), jnp.max(parts_q, 1), jnp.min(parts_k, 1), jnp.max(parts_k, 1)]
        ).astype(jnp.int32)

    bounds = [[limits(seg_blocks[0][b], seg_blocks[t][b]) for b in range(batch)] for t in range(n_seq)]
    seg_row = [seg_blocks[0][b][None, :] for b in range(batch)]
    seg_col = [[seg_blocks[t][b][:, None] for b in range(batch)] for t in range(n_seq)]

    queries = [(dot(hidden_blocks[0][b], weight_q, NN) + qv_bias[0]).astype(LOW) for b in range(batch)]
    keys, keys_t, values = [], [], []
    state = [()] * batch
    for t in range(n_seq):
        keys.append([])
        keys_t.append([])
        values.append([])
        for b in range(batch):
            key = dot(hidden_blocks[t][b], weight_k, NN).astype(LOW)
            value = (dot(hidden_blocks[t][b], weight_v, NN) + qv_bias[1]).astype(LOW)
            keys[t].append(key)
            keys_t[t].append(key.T)
            values[t].append(value)
            state[b] = attend(
                bounds[t][b], seg_row[b], seg_col[t][b], queries[b], key, value.T, tuple(state[b])
            )
    lse, context_full, context_low = [], [], []
    for b in range(batch):
        top, total, acc = state[b]
        lse.append(top + jnp.log2(jnp.where(total > 0, total, 1.0)))
        spread = jnp.broadcast_to(total[:heads, None, :], (heads, HEAD, local_len)).reshape(inner, -1)
        context_full.append((acc / spread).T)
        context_low.append(context_full[b].astype(LOW))
    context_sent = [
        jnp.concatenate([context_low[b][i * share : (i + 1) * share] for b in range(batch)], 0)
        for i in range(4)
    ]
    context = [context_sent[0]] + [flip(context_sent[i], "mp", FLIP[i]) for i in range(1, 4)]

    shard = jnp.concatenate([up_weight, down_weight, proj_weight], 1)
    pieces, positions = [shard], [s_at]
    for t in range(1, n_seq):
        pieces.append(onward(pieces[-1]))
        positions.append((s_at - t) % n_seq)
    seq_whole = place(pieces, positions)

    def over_dp(block):
        if halves:
            return jnp.concatenate([block, flip(block, "dp", 1)], 0)
        gathered = lax.all_gather(block, "dp", axis=0, tiled=True)
        return gathered

    near = over_dp(seq_whole)
    far = over_dp(flip(seq_whole, "mp", 2))
    blocks = [near, far, flip(near, "mp", 1), flip(far, "mp", 1)]
    ups = [block[:, :units] for block in blocks]
    downs = [block[:, units : 2 * units] for block in blocks]
    projs = [block[:, 2 * units :] for block in blocks]
    bias_far = flip(up_bias, "mp", 2)
    biases = [up_bias, bias_far, flip(up_bias, "mp", 1), flip(bias_far, "mp", 1)]

    attn = sum(dot(context[i], projs[i], NT) for i in range(4))
    hidden_own = own(hidden_in).astype(jnp.float32)
    first_in = hidden_own + swapped(attn) + proj_bias
    unit_one, first_back = jax.vjp(normalize, first_in)
    normed = unit_one * first_gain + first_shift
    normed_low = swapped(normed.astype(LOW))
    acts, slopes = [], []
    down = 0.0
    for i in range(4):
        pre = dot(normed_low, ups[i], NN) + biases[i]
        gate = 0.5 * (1.0 + lax.erf(pre * 0.7071067811865476))
        acts.append((pre * gate).astype(LOW))
        slopes.append(gate + pre * (0.3989422804014327 * jnp.exp(-0.5 * pre * pre)))
        down = down + dot(acts[i], downs[i], NT)
    second_in = normed + swapped(down) + down_bias
    unit_two, second_back = jax.vjp(normalize, second_in)
    out_own = (unit_two * second_gain + second_shift).astype(LOW)
    cot = own(cotangent).astype(jnp.float32)
    grad_second = second_back(cot * second_gain)[0]
    sums = [
        jnp.sum(grad_second, 0),
        jnp.sum(cot * unit_two, 0),
        jnp.sum(cot, 0),
    ]
    down_low = swapped(grad_second.astype(LOW))
    grads_up, grads_down, bias_sums = [], [], []
    normed_part = 0.0
    for i in range(4):
        pre_low = (dot(down_low, downs[i], NN) * slopes[i]).astype(LOW)
        bias_sums.append(jnp.sum(pre_low.astype(jnp.float32), 0))
        normed_part = normed_part + dot(pre_low, ups[i], NT)
        grads_up.append(dot(normed_low, pre_low, TN).astype(LOW))
        grads_down.append(dot(down_low, acts[i], TN).astype(LOW))
    grad_normed = grad_second + swapped(normed_part)
    grad_first = first_back(grad_normed * first_gain)[0]
    sums += [
        jnp.sum(grad_first, 0),
        jnp.sum(grad_normed * unit_one, 0),
        jnp.sum(grad_normed, 0),
    ]
    attn_low = swapped(grad_first.astype(LOW))
    grads_proj = [dot(attn_low, context[i], TN).astype(LOW) for i in range(4)]
    back = [dot(attn_low, projs[i], NN).astype(LOW) for i in range(4)]
    back = [back[0]] + [flip(back[i], "mp", FLIP[i]) for i in range(1, 4)]
    grad_context = [
        jnp.concatenate([back[i][b * share : (b + 1) * share] for i in range(4)], 0)
        for b in range(batch)
    ]

    def spread_rows(piece):
        parts = share_over_mp(piece)
        rows = piece.shape[0]
        return [parts[i * rows : (i + 1) * rows] for i in range(4)]

    def assemble(parts, dtype):
        whole = jnp.zeros((batch, local_len, width), dtype)
        for i in range(4):
            whole = lax.dynamic_update_slice_in_dim(
                whole, parts[i].reshape(batch, share, width).astype(dtype), (chunk_at ^ i) * share, 1
            )
        return whole

    layer_out = assemble(spread_rows(out_own), LOW)

    def owned_sum(grads):
        near = low_sum(grads[0], flip(grads[2], "mp", 1))
        far = low_sum(grads[1], flip(grads[3], "mp", 1))
        if halves:
            rows = near.shape[0] // 2
            near = low_sum(near[:rows], flip(near[rows:], "dp", 1))
            far = low_sum(far[:rows], flip(far[rows:], "dp", 1))
        else:
            near = lax.psum_scatter(near, "dp", scatter_dimension=0, tiled=True)
            far = lax.psum_scatter(far, "dp", scatter_dimension=0, tiled=True)
        return ring_sum(low_sum(near, flip(far, "mp", 2)))

    def ring_sum(rows):
        height = rows.shape[0] // n_seq
        total = None
        for t in range(1, n_seq + 1):
            part = lax.dynamic_slice_in_dim(rows, ((s_at - t) % n_seq) * height, height, 0)
            part = part.astype(jnp.float32)
            if total is not None:
                part = part + onward(total).astype(jnp.float32)
            total = part.astype(LOW)
        return part

    up_owned = owned_sum(grads_up)
    down_owned = owned_sum(grads_down)
    proj_owned = owned_sum(grads_proj)

    common = jnp.stack(sums)
    split = jnp.stack(bias_sums)
    small = jnp.concatenate([common.reshape(-1), split.reshape(-1)])
    cut = common.size
    far_small = flip(small, "mp", 2)
    common = small[:cut] + far_small[:cut]
    split = small[cut:].reshape(4, units)
    far_split = far_small[cut:].reshape(4, units)
    near_bias, next_bias = split[0] + far_split[1], split[2] + far_split[3]
    small = jnp.concatenate([common, next_bias])
    far_small = flip(small, "mp", 1)
    small = jnp.concatenate([common + far_small[:cut], near_bias + far_small[cut:]])

    def over_groups(value):
        for axis, size in (("dp", n_dp), ("seq", n_seq)):
            bit = 1
            while bit < size:
                value = value + flip(value, axis, bit)
                bit *= 2
        return value

    small = over_groups(small)
    norm_sums = small[:cut].reshape(-1, width)
    up_bias_grad = small[cut:]

    delta = []
    for b in range(batch):
        product = context_full[b] * grad_context[b].astype(jnp.float32)
        per_head = jnp.sum(product.reshape(local_len, heads, HEAD), -1)
        delta.append(jnp.pad(per_head.T, ((0, 8 - heads), (0, 0))))
    state = [()] * batch
    passing = [None] * batch
    grad_k = grad_v = grad_q = 0.0
    bias_q = bias_v = 0.0
    input_rows = [None] * batch
    for t in list(range(1, n_seq)) + [0]:
        for b in range(batch):
            dq, dk, dv = attend_back(
                bounds[t][b], seg_row[b], seg_col[t][b], queries[b], grad_context[b], lse[b], delta[b],
                keys[t][b], keys_t[t][b], values[t][b], tuple(state[b]),
            )
            state[b] = (dq,)
            bias_v = bias_v + jnp.sum(dv, 0)
            dk_low, dv_low = (dk * SCALE).astype(LOW), dv.astype(LOW)
            grad_k = grad_k + dot(hidden_blocks[t][b], dk_low, TN)
            grad_v = grad_v + dot(hidden_blocks[t][b], dv_low, TN)
            rows = dot(dk_low, weight_k, NT) + dot(dv_low, weight_v, NT)
            if t == 0:
                dq_low = (dq.T * SCALE).astype(LOW)
                bias_q = bias_q + jnp.sum(dq, 1) * SCALE
                grad_q = grad_q + dot(hidden_blocks[0][b], dq_low, TN)
                rows = rows + dot(dq_low, weight_q, NT)
            rows = sum_over_mp(rows.astype(LOW))
            if passing[b] is not None:
                rows = rows + onward(passing[b]).astype(jnp.float32)
            passing[b] = rows.astype(LOW)
            input_rows[b] = rows
    input_own = (grad_first + jnp.concatenate(input_rows, 0)).astype(LOW)
    input_grad = assemble(spread_rows(input_own), jnp.float32)
    grad_qkv = jnp.concatenate([grad_q, grad_k, grad_v], 1).astype(LOW)
    if halves:
        rows = width // 2
        mine = lax.dynamic_slice_in_dim(grad_qkv, d_at * rows, rows, 0)
        theirs = lax.dynamic_slice_in_dim(grad_qkv, (1 - d_at) * rows, rows, 0)
        grad_qkv = low_sum(mine, flip(theirs, "dp", 1))
    else:
        grad_qkv = lax.psum_scatter(grad_qkv, "dp", scatter_dimension=0, tiled=True)
    qkv_owned = ring_sum(grad_qkv).reshape(shard_rows, 3, inner)
    qv_bias_grad = over_groups(jnp.stack([bias_q, bias_v]))
    return (
        layer_out,
        input_grad,
        qkv_owned,
        qv_bias_grad,
        proj_owned,
        norm_sums[3],
        norm_sums[4],
        norm_sums[5],
        up_owned,
        up_bias_grad,
        down_owned,
        norm_sums[0],
        norm_sums[1],
        norm_sums[2],
    )


def solution(mesh):
    in_specs = (
        P("dp", "seq", None),
        P("dp", "seq"),
        P("dp", "seq", None),
        P(("dp", "seq"), None, "mp"),
        P(None, "mp"),
        P(("dp", "seq"), "mp"),
        P(),
        P(),
        P(),
        P(("dp", "seq"), "mp"),
        P("mp"),
        P(("dp", "seq"), "mp"),
        P(),
        P(),
        P(),
    )
    out_specs = (
        P("dp", "seq", None),
        P("dp", "seq", None),
        P(("dp", "seq"), None, "mp"),
        P(None, "mp"),
        P(("dp", "seq"), "mp"),
        P(),
        P(),
        P(),
        P(("dp", "seq"), "mp"),
        P("mp"),
        P(("dp", "seq"), "mp"),
        P(),
        P(),
        P(),
    )
    return jax.shard_map(shards, mesh=mesh, in_specs=in_specs, out_specs=out_specs, check_vma=False)
```

time: 1330 us -> 860 us (0.65); the launches traced: 1330 us -> 843 us
  matrix products: 497 us -> 149 us
  waiting for transfers between devices: 536 us -> 200 us
  local copies, waits for them, and re-layouts: 35.3 us -> 200 us
  blocking collectives: 166 us -> 17.3 us
  Pallas kernels: 0 us -> 108 us
  starting transfers between devices: 0.93 us -> 93.3 us
    psum x4 -> x0, waiting for transfers between devices: 368 us -> none  [head_total(): return lax.psum(partial_value, 'mp')]
    dot_general x34 -> x90, matrix products: 448 us -> 149 us  [dot(): lax.dot_general(left, right, dims, preferred_element_type=jnp.float32)]
    ppermute x0 -> x104, waiting for transfers between devices: none -> 200 us  [the longest x70 117 us: flip(): return lax.ppermute(value, axis, [(i, i ^ bit) for i in range(size)])]
    reduce_scatter x7 -> x0, waiting for transfers between devices: 157 us -> none  [the longest x1 72.4 us: shards(): lax.psum_scatter(acc_down, ('dp', 'seq'), scatter_dimension=0, tiled=True)]
    pallas_call x0 -> x16, Pallas kernels: none -> 108 us  [the longest x8 64.1 us: attend_back(): pl.pallas_call(functools.partial(bwd_body, not state), out_shape=(jax.Sha...]
    ppermute x0 -> x104, starting transfers between devices: none -> 93.3 us  [the longest x70 64.1 us: flip(): return lax.ppermute(value, axis, [(i, i ^ bit) for i in range(size)])]
    all_gather x4 -> x1, blocking collectives: 101 us -> 17.3 us  [shards(): lax.all_gather(seg_now.astype(LOW), 'seq', axis=0, tiled=False)]
    psum x2 -> x0, blocking collectives: 64.7 us -> none  [the longest x1 42.1 us: shards(): lax.psum((acc_pbias, acc_gain1, acc_shift1, acc_dbias, acc_gain2, acc_shi...]
  transfers between devices with their start and end apart: 18 -> 104, of which waited for: 8 -> 34; matrix products, arithmetic and copies ran while one was open for 37% -> 36% of each run, Pallas kernels for 0% -> 13%
where the time goes in v1:
time: 860 us; the launch traced here: 843 us
  local copies, waits for them, and re-layouts  200 us (23%)
  waiting for transfers between devices  200 us (23%)
  matrix products  149 us (17%)
  Pallas kernels  108 us (13%)
  starting transfers between devices  93.3 us (11%)
  other arithmetic  69.7 us (8%)
  blocking collectives  17.3 us (2%)
    dot_general x90, matrix products, dot(): lax.dot_general(left, right, dims, preferred_element_type=jnp.float32)  149 us
    ppermute x70, waiting for transfers between devices, flip(): return lax.ppermute(value, axis, [(i, i ^ bit) for i in range(size)])  117 us
    unnamed x555, local copies, waits for them, and re-layouts  94.3 us
    ppermute x27, waiting for transfers between devices, onward(): lax.ppermute(value, 'seq', [(i, (i + 1) % size) for i in range(size)])  82.9 us
    pallas_call x8, Pallas kernels, attend_back(): pl.pallas_call(functools.partial(bwd_body, not state), out_shape=(jax.Sha...  64.1 us
    ppermute x70, starting transfers between devices, flip(): return lax.ppermute(value, axis, [(i, i ^ bit) for i in range(size)])  64.1 us
    pallas_call x8, Pallas kernels, attend(): pl.pallas_call(functools.partial(fwd_body, not state), out_shape=(stats,...  44.3 us
    dynamic_update_slice x12, local copies, waits for them, and re-layouts, place(): whole = lax.dynamic_update_slice_in_dim(whole, piece, position * rows, 0)  43.6 us
  transfers between devices with their start and end apart: 104, of which 34 were waited for; matrix products, arithmetic and copies ran while one was open for 36% of the time, Pallas kernels for 13%

profile of v1, /device:TPU:0, one launch (start us, length us, event | category | flops | bytes accessed | tf_op | source)
XLA Modules:
  0.0 842.7 jit_solution(8459742475597032252)
XLA Ops:
  11.6 17.3 %all-gather.1 = bf16[4,2,1024]{2,1,0:T(2,128)(2,1)S(1)} all-gather(bf16[1,2,1024]{2,1,0:T(2,128)(2,1)S(1)} %get-tuple-element.273), channel_id=2, replica_groups=mesh['dp'=2,'seq'=4,'mp'=4] {'seq'}, dimensions={0}, use_global_device_ids=true | all-gather | bytes 20480 | tf_op jit(solution)/shard_map/all_gather | solution.py:247
  105.1 7.5 shard_map.254
  113.5 7.6 shard_map.258
  190.6 8.0 shard_map.255
  222.5 7.6 shard_map.256
  249.2 16.8 %collective-permute-done.31 = bf16[384,1728]{0,1:T(8,128)(2,1)S(1)} collective-permute-done((bf16[384,1728]{0,1:T(8,128)(2,1)}, bf16[384,1728]{0,1:T(8,128)(2,1)S(1)}, u32[]{:S(2)}, u32[]{:S(2)}) %collective-permute-start.31) | collective-permute-done | bytes 1327136 | tf_op jit(solution)/shard_map/ppermute | solution.py:155
  273.8 7.6 shard_map.257
  388.7 8.2 collective-permute-start.86
  416.4 8.0 collective-permute-done.43
  436.0 9.3 %shard_map.262 = (f32[192,1024]{1,0:T(8,128)S(1)}, f32[1024,192]{1,0:T(8,128)S(1)}, f32[1024,192]{1,0:T(8,128)S(1)}) custom-call(s32[4,2]{1,0:T(4,128)S(1)} %copy-done.128, f32[1,1024]{1,0:T(1,128)S(1)} %bitcast.240, f32[1024,1]{1,0:T(8,128)S(1)} %copy-done.29, bf16[1024,192]{1,0:T(8,128)(2,1)S(1)} %fusion.34.q, ...), custom_call_target="tpu_custom_call" | custom-call | tf_op jit(solution)/shard_map/pallas_call | solution.py:138
  450.4 10.3 %shard_map.263 = (f32[192,1024]{1,0:T(8,128)S(1)}, f32[1024,192]{1,0:T(8,128)S(1)}, f32[1024,192]{1,0:T(8,128)}) custom-call(s32[4,2]{1,0:T(4,128)S(1)} %copy-done.124, f32[1,1024]{1,0:T(1,128)S(1)} %bitcast.241, f32[1024,1]{1,0:T(8,128)S(1)} %copy-done.25, bf16[1024,192]{1,0:T(8,128)(2,1)S(1)} %fusion.34.q, bf16[1024,192]{1,0:T(8,128)(2,1)S(1)} %pad_maximum_fusion.12.do, ...), custom_call_target="tpu_custom_call" | custom-call | tf_op jit(solution)/shard_map/pallas_call | solution.py:138
  461.7 10.7 %shard_map.264 = (f32[192,1024]{1,0:T(8,128)S(1)}, f32[1024,192]{1,0:T(8,128)S(1)}, f32[1024,192]{1,0:T(8,128)}) custom-call(s32[4,2]{1,0:T(4,128)S(1)} %copy-done.122, f32[1,1024]{1,0:T(1,128)S(1)} %bitcast.242, f32[1024,1]{1,0:T(8,128)S(1)} %copy-done.23, bf16[1024,192]{1,0:T(8,128)(2,1)S(1)} %fusion.34.q, bf16[1024,192]{1,0:T(8,128)(2,1)S(1)} %pad_maximum_fusion.12.do, ...), custom_call_target="tpu_custom_call" | custom-call | tf_op jit(solution)/shard_map/pallas_call | solution.py:138
  473.5 10.4 %shard_map.265 = (f32[192,1024]{1,0:T(8,128)S(1)}, f32[1024,192]{1,0:T(8,128)S(1)}, f32[1024,192]{1,0:T(8,128)}) custom-call(s32[4,2]{1,0:T(4,128)S(1)} %copy-done.120, f32[1,1024]{1,0:T(1,128)S(1)} %bitcast.243, f32[1024,1]{1,0:T(8,128)S(1)} %copy-done.21, bf16[1024,192]{1,0:T(8,128)(2,1)S(1)} %fusion.34.q, bf16[1024,192]{1,0:T(8,128)(2,1)S(1)} %pad_maximum_fusion.12.do, ...), custom_call_target="tpu_custom_call" | custom-call | tf_op jit(solution)/shard_map/pallas_call | solution.py:138
  519.9 9.8 %shard_map.268 = (f32[192,1024]{1,0:T(8,128)S(1)}, f32[1024,192]{1,0:T(8,128)S(1)}, f32[1024,192]{1,0:T(8,128)}) custom-call(s32[4,2]{1,0:T(4,128)S(1)} %get-tuple-element.315.bounds, f32[1,1024]{1,0:T(1,128)S(1)} %bitcast.233, f32[1024,1]{1,0:T(8,128)S(1)} %copy-done.27, bf16[1024,192]{1,0:T(8,128)(2,1)S(1)} %fusion.39.q, ...), custom_call_target="tpu_custom_call" | custom-call | tf_op jit(solution)/shard_map/pallas_call | solution.py:138
  558.9 10.7 %shard_map.269 = (f32[192,1024]{1,0:T(8,128)S(1)}, f32[1024,192]{1,0:T(8,128)S(1)}, f32[1024,192]{1,0:T(8,128)}) custom-call(s32[4,2]{1,0:T(4,128)S(1)} %get-tuple-element.312.bounds, f32[1,1024]{1,0:T(1,128)S(1)} %bitcast.234, f32[1024,1]{1,0:T(8,128)S(1)} %copy-done.19, bf16[1024,192]{1,0:T(8,128)(2,1)S(1)} %fusion.39.q, ...), custom_call_target="tpu_custom_call" | custom-call | tf_op jit(solution)/shard_map/pallas_call | solution.py:138
  616.5 10.9 %collective-permute-start.73 = (f32[2,192]{1,0:T(2,128)S(1)}, f32[2,192]{1,0:T(2,128)S(1)}, u32[]{:S(2)}, u32[]{:S(2)}) collective-permute-start(f32[2,192]{1,0:T(2,128)S(1)} %fusion.182), channel_id=1, source_target_pairs={{0,4},{4,0},{8,12},{12,8},{1,5},{5,1},{9,13},{13,9},{2,6},{6,2},{1... | collective-permute-start | bytes 4616 | tf_op jit(solution)/shard_map/ppermute | solution.py:155
  713.6 9.1 %collective-permute-done.51 = bf16[256,768]{1,0:T(8,128)(2,1)S(1)} collective-permute-done((bf16[256,768]{1,0:T(8,128)(2,1)S(1)}, bf16[256,768]{1,0:T(8,128)(2,1)S(1)}, u32[]{:S(2)}, u32[]{:S(2)}) %collective-permute-start.51) | collective-permute-done | bytes 393248 | tf_op jit(solution)/shard_map/ppermute | solution.py:155
  723.4 15.7 %collective-permute-done.62 = bf16[256,768]{1,0:T(8,128)(2,1)S(1)} collective-permute-done((bf16[256,768]{1,0:T(8,128)(2,1)S(1)}, bf16[256,768]{1,0:T(8,128)(2,1)S(1)}, u32[]{:S(2)}, u32[]{:S(2)}) %collective-permute-start.62) | collective-permute-done | bytes 393248 | tf_op jit(solution)/shard_map/ppermute | solution.py:155
  740.1 12.9 %collective-permute-done.52 = bf16[256,768]{1,0:T(8,128)(2,1)S(1)} collective-permute-done((bf16[256,768]{1,0:T(8,128)(2,1)S(1)}, bf16[256,768]{1,0:T(8,128)(2,1)S(1)}, u32[]{:S(2)}, u32[]{:S(2)}) %collective-permute-start.52) | collective-permute-done | bytes 393248 | tf_op jit(solution)/shard_map/ppermute | solution.py:160
  761.9 12.0 %collective-permute-done.53 = bf16[256,768]{1,0:T(8,128)(2,1)S(1)} collective-permute-done((bf16[256,768]{1,0:T(8,128)(2,1)S(1)}, bf16[256,768]{1,0:T(8,128)(2,1)S(1)}, u32[]{:S(2)}, u32[]{:S(2)}) %collective-permute-start.53) | collective-permute-done | bytes 393248 | tf_op jit(solution)/shard_map/ppermute | solution.py:160
  782.6 7.6 collective-permute-done.92
  790.4 8.1 collective-permute-done.45
  808.3 14.5 %collective-permute-done.66 = bf16[512,768]{1,0:T(8,128)(2,1)S(1)} collective-permute-done((bf16[512,768]{1,0:T(8,128)(2,1)S(1)}, bf16[512,768]{1,0:T(8,128)(2,1)S(1)}, u32[]{:S(2)}, u32[]{:S(2)}) %collective-permute-start.66) | collective-permute-done | bytes 786464 | tf_op jit(solution)/shard_map/ppermute | solution.py:155
  824.5 7.0 collective-permute-done.94
  (1118 shorter events, 590.3 us)
Async XLA Ops:
  1.7 55.8 %collective-permute-start = (bf16[96,576]{0,1:T(8,128)(2,1)S(1)}, bf16[96,576]{0,1:T(8,128)(2,1)}, u32[]{:S(2)}, u32[]{:S(2)}) collective-permute-start(bf16[96,576]{0,1:T(8,128)(2,1)S(1)} %bitcast.253), channel_id=1, source_target_pairs={{0,4},{4,8},{8,12},{12,0},{16,20},{20,24},{24,28},{28,16},{1,5},{5... | collective-permute-start | bytes 331784 | tf_op jit(solution)/shard_map/ppermute | solution.py:239
  4.8 55.9 %collective-permute-start.1 = (bf16[96,576]{0,1:T(8,128)(2,1)S(1)}, bf16[96,576]{0,1:T(8,128)(2,1)}, u32[]{:S(2)}, u32[]{:S(2)}) collective-permute-start(bf16[96,576]{0,1:T(8,128)(2,1)S(1)} %bitcast.254), channel_id=1, source_target_pairs={{0,8},{4,12},{8,0},{12,4},{16,24},{20,28},{24,16},{28,20},{1,9},{5... | collective-permute-start | bytes 331784 | tf_op jit(solution)/shard_map/ppermute | solution.py:239
  7.4 62.2 %collective-permute-start.2 = (bf16[96,576]{0,1:T(8,128)(2,1)S(1)}, bf16[96,576]{0,1:T(8,128)(2,1)}, u32[]{:S(2)}, u32[]{:S(2)}) collective-permute-start(bf16[96,576]{0,1:T(8,128)(2,1)S(1)} %bitcast.255), channel_id=1, source_target_pairs={{0,12},{4,0},{8,4},{12,8},{16,28},{20,16},{24,20},{28,24},{1,13},{... | collective-permute-start | bytes 331784 | tf_op jit(solution)/shard_map/ppermute | solution.py:239
  8.7 63.9 %collective-permute-start.3 = (bf16[96,576]{0,1:T(8,128)(2,1)S(1)}, bf16[96,576]{0,1:T(8,128)(2,1)}, u32[]{:S(2)}, u32[]{:S(2)}) collective-permute-start(bf16[96,576]{0,1:T(8,128)(2,1)S(1)} %bitcast.256), channel_id=1, source_target_pairs={{0,16},{4,20},{8,24},{12,28},{16,0},{20,4},{24,8},{28,12},{1,17},{... | collective-permute-start | bytes 331784 | tf_op jit(solution)/shard_map/ppermute | solution.py:239
  10.2 65.6 %collective-permute-start.4 = (bf16[96,576]{0,1:T(8,128)(2,1)S(1)}, bf16[96,576]{0,1:T(8,128)(2,1)S(1)}, u32[]{:S(2)}, u32[]{:S(2)}) collective-permute-start(bf16[96,576]{0,1:T(8,128)(2,1)S(1)} %bitcast.257), channel_id=1, source_target_pairs={{0,20},{4,24},{8,28},{12,16},{16,4},{20,8},{24,12},{28,0},{1,21},{... | collective-permute-start | bytes 331784 | tf_op jit(solution)/shard_map/ppermute | solution.py:239
  75.8 52.1 %collective-permute-start.16 = (bf16[256,768]{1,0:T(8,128)(2,1)}, bf16[256,768]{1,0:T(8,128)(2,1)}, u32[]{:S(2)}, u32[]{:S(2)}) collective-permute-start(bf16[256,768]{1,0:T(8,128)(2,1)} %get-tuple-element.231), channel_id=1, source_target_pairs={{0,4},{4,8},{8,12},{12,0},{1,5},{5,9},{9,13},{13,1},{2,6},{6,10},{... | collective-permute-start | bytes 1179656 | tf_op jit(solution)/shard_map/ppermute | solution.py:160
  93.7 37.9 %collective-permute-start.26 = (bf16[96,1728]{0,1:T(8,128)(2,1)}, bf16[96,1728]{0,1:T(8,128)(2,1)}, u32[]{:S(2)}, u32[]{:S(2)}) collective-permute-start(bf16[96,1728]{0,1:T(8,128)(2,1)} %collective-permute-done.25), channel_id=1, source_target_pairs={{0,4},{4,8},{8,12},{12,0},{1,5},{5,9},{9,13},{13,1},{2,6},{6,10},{... | collective-permute-start | bytes 995336 | tf_op jit(solution)/shard_map/ppermute | solution.py:160
  96.0 44.7 %collective-permute-start.14 = (bf16[256,768]{1,0:T(8,128)(2,1)}, bf16[256,768]{1,0:T(8,128)(2,1)}, u32[]{:S(2)}, u32[]{:S(2)}) collective-permute-start(bf16[256,768]{1,0:T(8,128)(2,1)} %collective-permute-done.7), channel_id=1, source_target_pairs={{0,2},{1,3},{2,0},{3,1},{4,6},{5,7},{6,4},{7,5},{8,10},{9,11},{10,... | collective-permute-start | bytes 1179656 | tf_op jit(solution)/shard_map/ppermute | solution.py:155
  97.5 45.3 %collective-permute-start.8 = (bf16[256,768]{1,0:T(8,128)(2,1)}, bf16[256,768]{1,0:T(8,128)(2,1)}, u32[]{:S(2)}, u32[]{:S(2)}) collective-permute-start(bf16[256,768]{1,0:T(8,128)(2,1)} %collective-permute-done.7), channel_id=1, source_target_pairs={{0,4},{4,8},{8,12},{12,0},{1,5},{5,9},{9,13},{13,1},{2,6},{6,10},{... | collective-permute-start | bytes 1179656 | tf_op jit(solution)/shard_map/ppermute | solution.py:160
  153.8 79.5 %collective-permute-start.36 = (f32[768]{0:T(1024)}, f32[768]{0:T(1024)}, u32[]{:S(2)}, u32[]{:S(2)}) collective-permute-start(f32[768]{0:T(1024)} %param.25), channel_id=1, source_target_pairs={{0,2},{1,3},{2,0},{3,1},{4,6},{5,7},{6,4},{7,5},{8,10},{9,11},{10,... | collective-permute-start | bytes 9224 | tf_op jit(solution)/shard_map/ppermute | solution.py:155
  168.0 44.0 %collective-permute-start.13 = (bf16[512,768]{1,0:T(8,128)(2,1)}, bf16[512,768]{1,0:T(8,128)(2,1)}, u32[]{:S(2)}, u32[]{:S(2)}) collective-permute-start(bf16[512,768]{1,0:T(8,128)(2,1)} %pad_maximum_fusion.7), channel_id=1, source_target_pairs={{0,1},{1,0},{2,3},{3,2},{4,5},{5,4},{6,7},{7,6},{8,9},{9,8},{10,11... | collective-permute-start | bytes 2359304 | tf_op jit(solution)/shard_map/ppermute | solution.py:155
  233.3 91.3 %collective-permute-start.37 = (f32[768]{0:T(1024)}, f32[768]{0:T(1024)}, u32[]{:S(2)}, u32[]{:S(2)}) collective-permute-start(f32[768]{0:T(1024)} %param.25), channel_id=1, source_target_pairs={{0,1},{1,0},{2,3},{3,2},{4,5},{5,4},{6,7},{7,6},{8,9},{9,8},{10,11... | collective-permute-start | bytes 9224 | tf_op jit(solution)/shard_map/ppermute | solution.py:155
  233.9 97.6 %collective-permute-start.38 = (f32[768]{0:T(1024)}, f32[768]{0:T(1024)}, u32[]{:S(2)}, u32[]{:S(2)}) collective-permute-start(f32[768]{0:T(1024)} %collective-permute-done.36), channel_id=1, source_target_pairs={{0,1},{1,0},{2,3},{3,2},{4,5},{5,4},{6,7},{7,6},{8,9},{9,8},{10,11... | collective-permute-start | bytes 9224 | tf_op jit(solution)/shard_map/ppermute | solution.py:155
  243.5 64.0 %collective-permute-start.33 = (bf16[768,1728]{0,1:T(8,128)(2,1)}, bf16[768,1728]{0,1:T(8,128)(2,1)}, u32[]{:S(2)}, u32[]{:S(2)}) collective-permute-start(bf16[768,1728]{0,1:T(8,128)(2,1)} %pad_maximum_fusion), channel_id=1, source_target_pairs={{0,1},{1,0},{2,3},{3,2},{4,5},{5,4},{6,7},{7,6},{8,9},{9,8},{10,11... | collective-permute-start | bytes 7962632 | tf_op jit(solution)/shard_map/ppermute | solution.py:155
  267.2 47.9 %collective-permute-start.35 = (bf16[768,1728]{0,1:T(8,128)(2,1)}, bf16[768,1728]{0,1:T(8,128)(2,1)}, u32[]{:S(2)}, u32[]{:S(2)}) collective-permute-start(bf16[768,1728]{0,1:T(8,128)(2,1)} %constant_dynamic-update-slice_fusion.18), channel_id=1, source_target_pairs={{0,1},{1,0},{2,3},{3,2},{4,5},{5,4},{6,7},{7,6},{8,9},{9,8},{10,11... | collective-permute-start | bytes 7962632 | tf_op jit(solution)/shard_map/ppermute | solution.py:155
  375.0 328.6 %collective-permute-start.96 = (bf16[768,768]{1,0:T(8,128)(2,1)}, bf16[768,768]{1,0:T(8,128)(2,1)}, u32[]{:S(2)}, u32[]{:S(2)}) collective-permute-start(bf16[768,768]{1,0:T(8,128)(2,1)} %convolution_convert_fusion.2), channel_id=1, source_target_pairs={{0,1},{1,0},{2,3},{3,2},{4,5},{5,4},{6,7},{7,6},{8,9},{9,8},{10,11... | collective-permute-start | bytes 3538952 | tf_op jit(solution)/shard_map/ppermute | solution.py:155
  377.2 251.9 %collective-permute-start.75 = (bf16[768,192]{0,1:T(8,128)(2,1)}, bf16[768,192]{0,1:T(8,128)(2,1)}, u32[]{:S(2)}, u32[]{:S(2)}) collective-permute-start(bf16[768,192]{0,1:T(8,128)(2,1)} %convolution_convert_fusion.18), channel_id=1, source_target_pairs={{0,1},{1,0},{2,3},{3,2},{4,5},{5,4},{6,7},{7,6},{8,9},{9,8},{10,11... | collective-permute-start | bytes 884744 | tf_op jit(solution)/shard_map/ppermute | solution.py:155
  378.5 238.0 %collective-permute-start.77 = (bf16[768,192]{0,1:T(8,128)(2,1)}, bf16[768,192]{0,1:T(8,128)(2,1)}, u32[]{:S(2)}, u32[]{:S(2)}) collective-permute-start(bf16[768,192]{0,1:T(8,128)(2,1)} %convolution_convert_fusion.16), channel_id=1, source_target_pairs={{0,1},{1,0},{2,3},{3,2},{4,5},{5,4},{6,7},{7,6},{8,9},{9,8},{10,11... | collective-permute-start | bytes 884744 | tf_op jit(solution)/shard_map/ppermute | solution.py:155
  379.0 296.7 %collective-permute-start.39 = (bf16[512,768]{1,0:T(8,128)(2,1)}, bf16[512,768]{1,0:T(8,128)(2,1)}, u32[]{:S(2)}, u32[]{:S(2)}) collective-permute-start(bf16[512,768]{1,0:T(8,128)(2,1)} %get-tuple-element.212), channel_id=1, source_target_pairs={{0,2},{1,3},{2,0},{3,1},{4,6},{5,7},{6,4},{7,5},{8,10},{9,11},{10,... | collective-permute-start | bytes 2359304 | tf_op jit(solution)/shard_map/ppermute | solution.py:155
  615.5 41.1 %collective-permute-start.68 = (bf16[384,576]{0,1:T(8,128)(2,1)S(1)}, bf16[384,576]{0,1:T(8,128)(2,1)S(1)}, u32[]{:S(2)}, u32[]{:S(2)}) collective-permute-start(bf16[384,576]{0,1:T(8,128)(2,1)S(1)} %constant_dynamic-slice_fusion.7), channel_id=1, source_target_pairs={{0,16},{16,0},{1,17},{17,1},{2,18},{18,2},{3,19},{19,3},{4,20},{20... | collective-permute-start | bytes 1327112 | tf_op jit(solution)/shard_map/ppermute | solution.py:155
  655.3 51.5 %collective-permute-start.98 = (bf16[768,768]{1,0:T(8,128)(2,1)}, bf16[768,768]{1,0:T(8,128)(2,1)}, u32[]{:S(2)}, u32[]{:S(2)}) collective-permute-start(bf16[768,768]{1,0:T(8,128)(2,1)} %convolution_convert_fusion), channel_id=1, source_target_pairs={{0,1},{1,0},{2,3},{3,2},{4,5},{5,4},{6,7},{7,6},{8,9},{9,8},{10,11... | collective-permute-start | bytes 3538952 | tf_op jit(solution)/shard_map/ppermute | solution.py:155
  702.3 37.1 %collective-permute-start.49 = (bf16[256,768]{1,0:T(8,128)(2,1)S(1)}, bf16[256,768]{1,0:T(8,128)(2,1)S(1)}, u32[]{:S(2)}, u32[]{:S(2)}) collective-permute-start(bf16[256,768]{1,0:T(8,128)(2,1)S(1)} %slice.497), channel_id=1, source_target_pairs={{0,2},{1,3},{2,0},{3,1},{4,6},{5,7},{6,4},{7,5},{8,10},{9,11},{10,... | collective-permute-start | bytes 1179656 | tf_op jit(solution)/shard_map/ppermute | solution.py:155
  706.9 46.8 %collective-permute-start.60 = (bf16[256,768]{1,0:T(8,128)(2,1)S(1)}, bf16[256,768]{1,0:T(8,128)(2,1)S(1)}, u32[]{:S(2)}, u32[]{:S(2)}) collective-permute-start(bf16[256,768]{1,0:T(8,128)(2,1)S(1)} %slice.517), channel_id=1, source_target_pairs={{0,2},{1,3},{2,0},{3,1},{4,6},{5,7},{6,4},{7,5},{8,10},{9,11},{10,... | collective-permute-start | bytes 1179656 | tf_op jit(solution)/shard_map/ppermute | solution.py:155
  722.7 38.1 %collective-permute-start.91 = (bf16[384,768]{1,0:T(8,128)(2,1)S(1)}, bf16[384,768]{1,0:T(8,128)(2,1)S(1)}, u32[]{:S(2)}, u32[]{:S(2)}) collective-permute-start(bf16[384,768]{1,0:T(8,128)(2,1)S(1)} %slice.539), channel_id=1, source_target_pairs={{0,16},{16,0},{1,17},{17,1},{2,18},{18,2},{3,19},{19,3},{4,20},{20... | collective-permute-start | bytes 1769480 | tf_op jit(solution)/shard_map/ppermute | solution.py:155
  (348 other events, 2979.6 us)

commit v2 on v1

v2 whole, which is shorter than its diff:
```python
import functools

import jax
import jax.numpy as jnp
from jax import lax
from jax.experimental import pallas as pl
from jax.experimental.pallas import tpu as pltpu
from jax.sharding import PartitionSpec as P

HEAD = 64
EPS = 1e-06
SCALE = HEAD**-0.5
LOG2E = 1.4426950408889634
CEXP = LOG2E * SCALE
QB = 512
KB = 512
NT = (((1,), (1,)), ((), ()))
NN = (((1,), (0,)), ((), ()))
VMEM = pl.BlockSpec(memory_space=pltpu.VMEM)
SMEM = pl.BlockSpec(memory_space=pltpu.SMEM)
LOW = jnp.bfloat16
F32 = jnp.float32
FLIP = (0, 2, 1, 3)


def dot(left, right, dims):
    return lax.dot_general(left, right, dims, preferred_element_type=F32)


def struct(shape, dtype):
    return jax.ShapeDtypeStruct(shape, dtype)


def call(body, ins, outs, scratch, mib, scalars=1):
    return pl.pallas_call(
        body,
        out_shape=tuple(outs),
        in_specs=[SMEM] * scalars + [VMEM] * (len(ins) - scalars),
        out_specs=(VMEM,) * len(outs),
        scratch_shapes=scratch,
        compiler_params=pltpu.CompilerParams(vmem_limit_bytes=mib * 2**20),
    )(*ins)


def visit(bounds, qi, kj, work):
    qlo, qhi, klo, khi = bounds[0, qi], bounds[1, qi], bounds[2, kj], bounds[3, kj]
    overlap = (qlo <= khi) & (klo <= qhi)
    pure = (qlo == qhi) & (klo == khi) & (qlo == klo)
    pl.when(pure)(lambda: work(False))
    pl.when(overlap & jnp.logical_not(pure))(lambda: work(True))


def fill(target, pieces):
    rows = pieces[0].shape[0]
    for i, piece in enumerate(pieces):
        target[i * rows : (i + 1) * rows, :] = piece[...]


def segment_column(target, segk):
    target[...] = jnp.broadcast_to(segk[...], (128, segk.shape[1])).T


def fwd_body(first, last, bounds, segq, segk, *refs):
    refs = list(refs)
    pieces = [refs.pop(0) for _ in range(4)]
    wkv, vbias = refs.pop(0), refs.pop(0)
    if first:
        wq, qbias = refs.pop(0), refs.pop(0)
        before = None
    else:
        q = refs.pop(0)
        before = [refs.pop(0) for _ in range(3)]
    kv = refs.pop(0)
    if first:
        q = refs.pop(0)
    if last:
        contexts = [refs.pop(0) for _ in range(4)]
        out_t, lse = refs.pop(0), refs.pop(0)
    top, total, acc = refs.pop(0), refs.pop(0), refs.pop(0)
    hidden, vt, segc = refs
    inner = q.shape[1]
    fill(hidden, pieces)
    segment_column(segc, segk)
    value = dot(hidden[...], wkv[...], NN)
    kv[:, :inner] = value[:, :inner].astype(LOW)
    value = value[:, inner:] + vbias[...]
    kv[:, inner:] = value.astype(LOW)
    vt[...] = value.T.astype(LOW)
    if first:
        q[...] = (dot(hidden[...], wq[...], NN) + qbias[...]).astype(LOW)
        top[...] = jnp.full(top.shape, -1e30, F32)
        total[...] = jnp.zeros(total.shape, F32)
        acc[...] = jnp.zeros(acc.shape, F32)
    else:
        top[...], total[...], acc[...] = (ref[...] for ref in before)

    def qstep(qi, _):
        qs = pl.ds(pl.multiple_of(qi * QB, QB), QB)

        def kstep(kj, _):
            ks = pl.ds(pl.multiple_of(kj * KB, KB), KB)

            def work(masked):
                if masked:
                    bad = segc[ks, 0:1] != segq[0:1, qs]
                for h in range(inner // HEAD):
                    c = slice(h * HEAD, (h + 1) * HEAD)
                    s = dot(kv[ks, c], q[qs, c], NT) * CEXP
                    if masked:
                        s = jnp.where(bad, -1e30, s)
                    old = top[h : h + 1, qs]
                    new = jnp.maximum(old, jnp.max(s, 0, keepdims=True))
                    p = jnp.exp2(s - new)
                    shrink = jnp.exp2(old - new)
                    top[h : h + 1, qs] = new
                    total[h : h + 1, qs] = total[h : h + 1, qs] * shrink + jnp.sum(p, 0, keepdims=True)
                    acc[c, qs] = acc[c, qs] * shrink + dot(vt[c, ks], p.astype(LOW), NN)

            visit(bounds, qi, kj, work)
            return 0

        lax.fori_loop(0, kv.shape[0] // KB, kstep, 0)
        return 0

    lax.fori_loop(0, q.shape[0] // QB, qstep, 0)
    if last:
        for h in range(inner // HEAD):
            c = slice(h * HEAD, (h + 1) * HEAD)
            out_t[c, :] = acc[c, :] / total[h : h + 1, :]
            lse[h : h + 1, :] = top[h : h + 1, :] + jnp.log(total[h : h + 1, :]) * LOG2E
        natural = out_t[...].T.astype(LOW)
        rows = contexts[0].shape[0]
        for i in range(4):
            contexts[i][...] = natural[i * rows : (i + 1) * rows, :]


def attend(first, last, bounds, segq, segk, pieces, wkv, vbias, more):
    rows = 4 * pieces[0].shape[0]
    width, inner = wkv.shape[0], wkv.shape[1] // 2
    stats = [((8, rows), F32), ((8, rows), F32), ((inner, rows), F32)]
    outs = [struct((rows, 2 * inner), LOW)]
    if first:
        outs.append(struct((rows, inner), LOW))
    if last:
        outs += [struct((rows // 4, inner), LOW)] * 4 + [struct((inner, rows), F32), struct((8, rows), F32)]
    else:
        outs += [struct(*item) for item in stats]
    scratch = [pltpu.VMEM(*item) for item in stats] if last else []
    scratch += [pltpu.VMEM((rows, width), LOW), pltpu.VMEM((inner, rows), LOW), pltpu.VMEM((rows, 128), F32)]
    ins = [bounds, segq, segk, *pieces, wkv, vbias, *more]
    return call(functools.partial(fwd_body, first, last), ins, outs, scratch, 24)


def bwd_body(first, last, add, bounds, segq, segk, *refs):
    refs = list(refs)
    pieces = [refs.pop(0) for _ in range(4)]
    back = [refs.pop(0) for _ in range(4)]
    wkv, q, kv, lse, extra = (refs.pop(0) for _ in range(5))
    if not first:
        dq_before = refs.pop(0)
    if add:
        gkv_before = refs.pop(0)
    if last:
        wq = refs.pop(0)
    keep, send, gkv, vsum = (refs.pop(0) for _ in range(4))
    if first:
        delta = refs.pop(0)
    else:
        delta = extra
    if last:
        gq, qsum = refs.pop(0), refs.pop(0)
    dq = refs.pop(0)
    hidden, do, kt, segc, dk, dv, dkv = refs
    inner = q.shape[1]
    fill(hidden, pieces)
    fill(do, back)
    segment_column(segc, segk)
    kt[...] = kv[:, :inner].astype(F32).T.astype(LOW)
    if first:
        product = do[...].astype(F32).T * extra[...]
        delta[...] = jnp.zeros(delta.shape, F32)
        for h in range(inner // HEAD):
            delta[h : h + 1, :] = jnp.sum(product[h * HEAD : (h + 1) * HEAD, :], 0, keepdims=True)
        dq[...] = jnp.zeros(dq.shape, F32)
    else:
        dq[...] = dq_before[...]
    dk[...] = jnp.zeros(dk.shape, F32)
    dv[...] = jnp.zeros(dv.shape, F32)

    def kstep(kj, _):
        ks = pl.ds(pl.multiple_of(kj * KB, KB), KB)

        def qstep(qi, _):
            qs = pl.ds(pl.multiple_of(qi * QB, QB), QB)

            def work(masked):
                if masked:
                    bad = segc[ks, 0:1] != segq[0:1, qs]
                for h in range(inner // HEAD):
                    c = slice(h * HEAD, (h + 1) * HEAD)
                    cv = slice(inner + h * HEAD, inner + (h + 1) * HEAD)
                    qh = q[qs, c]
                    dh = do[qs, c]
                    s = dot(kv[ks, c], qh, NT) * CEXP - lse[h : h + 1, qs]
                    if masked:
                        s = jnp.where(bad, -1e30, s)
                    p = jnp.exp2(s)
                    dp = dot(kv[ks, cv], dh, NT)
                    ds = (p * (dp - delta[h : h + 1, qs])).astype(LOW)
                    dv[ks, c] += dot(p.astype(LOW), dh, NN)
                    dk[ks, c] += dot(ds, qh, NN)
                    dq[c, qs] += dot(kt[c, ks], ds, NN)

            visit(bounds, qi, kj, work)
            return 0

        lax.fori_loop(0, q.shape[0] // QB, qstep, 0)
        return 0

    lax.fori_loop(0, kv.shape[0] // KB, kstep, 0)
    dkv[:, :inner] = (dk[...] * SCALE).astype(LOW)
    dkv[:, inner:] = dv[...].astype(LOW)
    vsum[...] = jnp.broadcast_to(jnp.sum(dv[...], 0, keepdims=True), vsum.shape)
    half = keep.shape[0]
    if last:
        dq_low = (dq[...] * SCALE).T
        qsum[...] = jnp.broadcast_to(jnp.sum(dq_low, 0, keepdims=True), qsum.shape)
        dq_low = dq_low.astype(LOW)
        gq[...] = dot((dq[...] * SCALE).astype(LOW), hidden[...], NN)
    for part, out in ((slice(0, half), keep), (slice(half, 2 * half), send)):
        value = dot(dkv[part, :], wkv[...], NT)
        if last:
            value = value + dot(dq_low[part, :], wq[...], NT)
        out[...] = value.astype(LOW)
    parts = [(dk[...] * SCALE).T.astype(LOW), dv[...].T.astype(LOW)]
    for i in range(2):
        rows = slice(i * inner, (i + 1) * inner)
        value = dot(parts[i], hidden[...], NN)
        gkv[rows, :] = gkv_before[rows, :] + value if add else value


def attend_back(first, last, bounds, segq, segk, pieces, back, wkv, q, kv, lse, extra, dq, gkv, wq):
    rows, inner = q.shape
    width = wkv.shape[0]
    outs = [struct((rows // 2, width), LOW)] * 2 + [struct((2 * inner, width), F32), struct((8, inner), F32)]
    if first:
        outs.append(struct((8, rows), F32))
    if last:
        outs += [struct((inner, width), F32), struct((8, inner), F32)]
    scratch = []
    if last:
        scratch.append(pltpu.VMEM((inner, rows), F32))
    else:
        outs.append(struct((inner, rows), F32))
    scratch += [
        pltpu.VMEM((rows, width), LOW),
        pltpu.VMEM((rows, inner), LOW),
        pltpu.VMEM((inner, rows), LOW),
        pltpu.VMEM((rows, 128), F32),
        pltpu.VMEM((rows, inner), F32),
        pltpu.VMEM((rows, inner), F32),
        pltpu.VMEM((rows, 2 * inner), LOW),
    ]
    ins = [bounds, segq, segk, *pieces, *back, wkv, q, kv, lse, extra]
    ins += [] if first else [dq]
    ins += [] if gkv is None else [gkv]
    ins += [wq] if last else []
    return call(functools.partial(bwd_body, first, last, gkv is not None), ins, outs, scratch, 28)


def rows_body(halves, batch, flag, *refs):
    refs = list(refs)
    take = lambda count: [refs.pop(0) for _ in range(count)]
    ctx_in = take(4 * batch)
    hidden, cot, vec, bias = take(4)
    low_w, high_w = take(4), take(4)
    out_low, grad_first, sums, bias_sums = take(4)
    back = take(4 * batch)
    acts, pres, ctxs = take(4), take(4), take(4)
    nl_t, dl_t, al_t = take(3)
    slopes = take(4)
    width = hidden.shape[1]
    half = width // 2
    units = (low_w[0].shape[1] - ctxs[0].shape[1]) // 2
    up, down, proj = slice(0, units), slice(units, 2 * units), slice(2 * units, low_w[0].shape[1])

    def swapped(value):
        if not halves:
            return value
        turned = jnp.concatenate([value[:, half:], value[:, :half]], 1)
        return jnp.where(flag[0] == 1, turned, value)

    def into(value, r, cols):
        return dot(value[:, :half], low_w[r][:, cols], NN) + dot(value[:, half:], high_w[r][:, cols], NN)

    def out_of(value, r, cols):
        return jnp.concatenate([dot(value, low_w[r][:, cols], NT), dot(value, high_w[r][:, cols], NT)], 1)

    def norm(value):
        center = value - jnp.mean(value, -1, keepdims=True)
        inverse = lax.rsqrt(jnp.mean(center * center, -1, keepdims=True) + EPS)
        return center * inverse, inverse

    def norm_back(grad, unit, inverse):
        shared = jnp.mean(grad, -1, keepdims=True)
        return inverse * (grad - shared - unit * jnp.mean(grad * unit, -1, keepdims=True))

    attn = None
    for r in range(4):
        fill(ctxs[r], [ctx_in[b * 4 + r] for b in range(batch)])
        part = out_of(ctxs[r][...], r, proj)
        attn = part if attn is None else attn + part
    unit_one, inverse_one = norm(hidden[...].astype(F32) + swapped(attn) + vec[0:1, :])
    normed = unit_one * vec[1:2, :] + vec[2:3, :]
    normed_sw = swapped(normed)
    nl_t[...] = normed_sw.T.astype(LOW)
    normed_low = normed_sw.astype(LOW)
    total = None
    for r in range(4):
        pre = into(normed_low, r, up) + bias[r : r + 1, :]
        gate = 0.5 + 0.5 * lax.erf(pre * 0.7071067811865476)
        acts[r][...] = (pre * gate).astype(LOW)
        slopes[r][...] = gate + pre * (0.3989422804014327 * jnp.exp(-0.5 * pre * pre))
        part = out_of(acts[r][...], r, down)
        total = part if total is None else total + part
    unit_two, inverse_two = norm(normed + swapped(total) + vec[3:4, :])
    out_low[...] = (unit_two * vec[4:5, :] + vec[5:6, :]).astype(LOW)
    cotangent = cot[...].astype(F32)
    grad_second = norm_back(cotangent * vec[4:5, :], unit_two, inverse_two)
    sums[...] = jnp.zeros(sums.shape, F32)
    sums[0:1, :] = jnp.sum(grad_second, 0, keepdims=True)
    sums[1:2, :] = jnp.sum(cotangent * unit_two, 0, keepdims=True)
    sums[2:3, :] = jnp.sum(cotangent, 0, keepdims=True)
    second_sw = swapped(grad_second)
    dl_t[...] = second_sw.T.astype(LOW)
    down_low = second_sw.astype(LOW)
    total = None
    for r in range(4):
        pre_low = (into(down_low, r, down) * slopes[r][...]).astype(LOW)
        pres[r][...] = pre_low
        bias_sums[r : r + 1, :] = jnp.sum(pre_low.astype(F32), 0, keepdims=True)
        part = out_of(pre_low, r, up)
        total = part if total is None else total + part
    grad_normed = grad_second + swapped(total)
    first = norm_back(grad_normed * vec[1:2, :], unit_one, inverse_one)
    grad_first[...] = first
    sums[3:4, :] = jnp.sum(first, 0, keepdims=True)
    sums[4:5, :] = jnp.sum(grad_normed * unit_one, 0, keepdims=True)
    sums[5:6, :] = jnp.sum(grad_normed, 0, keepdims=True)
    first_sw = swapped(first)
    al_t[...] = first_sw.T.astype(LOW)
    attn_low = first_sw.astype(LOW)
    share = back[0].shape[0]
    for r in range(4):
        value = into(attn_low, r, proj).astype(LOW)
        for b in range(batch):
            back[b * 4 + r][...] = value[b * share : (b + 1) * share, :]


def own_rows_pass(halves, batch, flag, ctx, hidden, cot, vec, bias, low_w, high_w):
    rows, width = hidden.shape
    share, inner = ctx[0].shape
    units = bias.shape[1]
    outs = [struct((rows, width), LOW), struct((rows, width), F32), struct((8, width), F32), struct((4, units), F32)]
    outs += [struct((share, inner), LOW)] * (4 * batch)
    outs += [struct((rows, units), LOW)] * 8 + [struct((rows, inner), LOW)] * 4
    outs += [struct((width, rows), LOW)] * 3
    ins = [flag, *ctx, hidden, cot, vec, bias, *low_w, *high_w]
    scratch = [pltpu.VMEM((rows, units), F32)] * 4
    return call(functools.partial(rows_body, halves, batch), ins, outs, scratch, 40)


def grads_body(nl_t, dl_t, al_t, pre, act, ctx, out):
    units = act.shape[1]
    out[:, :units] = dot(nl_t[...], pre[...], NN).astype(LOW)
    out[:, units : 2 * units] = dot(dl_t[...], act[...], NN).astype(LOW)
    out[:, 2 * units :] = dot(al_t[...], ctx[...], NN).astype(LOW)


def weight_grads(nl_t, dl_t, al_t, pre, act, ctx):
    shape = (nl_t.shape[0], 2 * act.shape[1] + ctx.shape[1])
    return call(grads_body, [nl_t, dl_t, al_t, pre, act, ctx], [struct(shape, LOW)], [], 20, 0)[0]


def flip(value, axis, bit):
    size = lax.axis_size(axis)
    return lax.ppermute(value, axis, [(i, i ^ bit) for i in range(size)])


def onward(value, step=1):
    size = lax.axis_size("seq")
    return lax.ppermute(value, "seq", [(i, (i + step) % size) for i in range(size)])


def after(value, *others):
    return lax.optimization_barrier((value,) + others)[0]


def low_sum(left, right):
    return (left.astype(F32) + right.astype(F32)).astype(LOW)


def shards(
    hidden_in,
    segments,
    cotangent,
    qkv_weight,
    qv_bias,
    proj_weight,
    proj_bias,
    first_gain,
    first_shift,
    up_weight,
    up_bias,
    down_weight,
    down_bias,
    second_gain,
    second_shift,
):
    batch, local_len, width = hidden_in.shape
    inner = qkv_weight.shape[2]
    n_dp, n_seq, n_mp = lax.axis_size("dp"), lax.axis_size("seq"), lax.axis_size("mp")
    assert n_mp == 4
    d_at, s_at, m_at = lax.axis_index("dp"), lax.axis_index("seq"), lax.axis_index("mp")
    chunk_at = (m_at % 2) * 2 + m_at // 2
    share = local_len // n_mp
    shard_rows = qkv_weight.shape[0]
    halves = n_dp == 2

    def place(pieces, positions):
        whole = jnp.zeros((len(pieces),) + pieces[0].shape, pieces[0].dtype)
        for piece, position in zip(pieces, positions):
            whole = lax.dynamic_update_index_in_dim(whole, piece, position, 0)
        return whole.reshape((-1,) + pieces[0].shape[1:])

    def chunk(rows, i):
        parts = rows.reshape((4, share) + rows.shape[1:])
        return lax.dynamic_index_in_dim(parts, chunk_at ^ i, 0, keepdims=False)

    def own(rows):
        return jnp.concatenate([chunk(rows[b], 0) for b in range(batch)], 0)

    flat_qkv = qkv_weight.reshape(shard_rows, 3 * inner)
    if halves:
        pieces, positions = [flat_qkv], [d_at * n_seq + s_at]
        for dy in range(2):
            for dz in range(n_seq):
                if dy or dz:
                    pairs = [
                        (y * n_seq + z, (y ^ dy) * n_seq + (z + dz) % n_seq)
                        for y in range(2)
                        for z in range(n_seq)
                    ]
                    pieces.append(lax.ppermute(flat_qkv, ("dp", "seq"), pairs))
                    positions.append((d_at ^ dy) * n_seq + (s_at - dz) % n_seq)
        full_qkv = place(pieces, positions)
    else:
        full_qkv = lax.all_gather(flat_qkv, ("dp", "seq"), axis=0, tiled=True)
    weight_q, weight_kv = full_qkv[:, :inner], full_qkv[:, inner:]
    bias_q, bias_v = qv_bias[0:1], qv_bias[1:2]

    seg_all = [segments] + [onward(segments, t) for t in range(1, n_seq)]
    hidden_blocks = [[[chunk(hidden_in[b], i) for i in range(4)] for b in range(batch)]]
    seg_blocks = [
        [jnp.concatenate([chunk(seg_all[t][b], i) for i in range(4)], 0) for b in range(batch)]
        for t in range(n_seq)
    ]
    shard = jnp.concatenate([up_weight, down_weight, proj_weight], 1)
    shard_pieces = [shard] + [onward(shard, t) for t in range(1, n_seq)]

    def share_over_mp(piece):
        across = flip(piece, "mp", 2)
        return [piece, across, flip(piece, "mp", 1), flip(across, "mp", 1)]

    arrived = {}
    for b in range(batch):
        for t in range(1, n_seq):
            piece = hidden_blocks[0][b][0]
            if b:
                piece = after(piece, arrived[0, n_seq - 1])
            arrived[b, t] = onward(piece, t)
    for t in range(1, n_seq):
        hidden_blocks.append([share_over_mp(arrived[b, t]) for b in range(batch)])

    def limits(queries, keys):
        parts_q, parts_k = queries.reshape(-1, QB), keys.reshape(-1, KB)
        return jnp.stack([jnp.min(parts_q, 1), jnp.max(parts_q, 1), jnp.min(parts_k, 1), jnp.max(parts_k, 1)])

    bounds = [[limits(seg_blocks[0][b], seg_blocks[t][b]) for b in range(batch)] for t in range(n_seq)]
    seg_rows = [[seg_blocks[t][b].astype(F32)[None, :] for b in range(batch)] for t in range(n_seq)]

    seq_whole = place(shard_pieces, [(s_at - t) % n_seq for t in range(n_seq)])

    def over_dp(block):
        if halves:
            return block, flip(block, "dp", 1)
        return tuple(jnp.split(lax.all_gather(block, "dp", axis=0, tiled=True), 2, 0))

    near_low, near_high = over_dp(seq_whole)
    far_low, far_high = over_dp(flip(seq_whole, "mp", 2))
    low_w = [near_low, far_low, flip(near_low, "mp", 1), flip(far_low, "mp", 1)]
    high_w = [near_high, far_high, flip(near_high, "mp", 1), flip(far_high, "mp", 1)]
    up_bias_row = up_bias[None, :]
    bias_far = flip(up_bias_row, "mp", 2)
    biases = jnp.concatenate([up_bias_row, bias_far, flip(up_bias_row, "mp", 1), flip(bias_far, "mp", 1)], 0)

    queries = [None] * batch
    key_values = [[None] * batch for _ in range(n_seq)]
    state = [None] * batch
    contexts = []
    lse, out_t = [None] * batch, [None] * batch
    order = [(0, b) for b in range(batch)] + [(t, b) for b in range(batch) for t in range(1, n_seq)]
    token = None
    for t, b in order:
        first, last = t == 0, t == n_seq - 1
        segk = seg_rows[t][b]
        if token is not None:
            segk = after(segk, token)
        more = (weight_q, bias_q) if first else (queries[b], *state[b])
        outs = list(
            attend(first, last, bounds[t][b], seg_rows[0][b], segk, hidden_blocks[t][b], weight_kv, bias_v, more)
        )
        token = key_values[t][b] = outs.pop(0)
        if first:
            queries[b] = outs.pop(0)
        if last:
            contexts.append([outs[0]] + [flip(outs[i], "mp", FLIP[i]) for i in range(1, 4)])
            out_t[b], lse[b] = outs[4:]
        else:
            state[b] = outs

    vec = jnp.stack([proj_bias, first_gain, first_shift, down_bias, second_gain, second_shift])
    outs = list(
        own_rows_pass(
            halves, batch, d_at.astype(jnp.int32)[None], [c for cs in contexts for c in cs],
            own(hidden_in), own(cotangent), vec, biases, low_w, high_w,
        )
    )
    out_own, grad_first, sums, bias_sums = outs[:4]
    back, outs = outs[4 : 4 + 4 * batch], outs[4 + 4 * batch :]
    acts, pres, ctxs, transposed = outs[:4], outs[4:8], outs[8:12], outs[12:]
    back = [
        [back[b * 4]] + [flip(back[b * 4 + i], "mp", FLIP[i]) for i in range(1, 4)] for b in range(batch)
    ]
    grads = [None] * 4
    for i in (2, 3, 0, 1):
        grads[i] = weight_grads(*transposed, pres[i], acts[i], ctxs[i])

    def assemble(parts, dtype):
        whole = jnp.zeros((4, share, width), dtype)
        for i in range(4):
            whole = lax.dynamic_update_index_in_dim(whole, parts[i].astype(dtype), chunk_at ^ i, 0)
        return whole.reshape(1, local_len, width)

    def ring_sum(rows):
        parts = rows.reshape((n_seq, -1) + rows.shape[1:])
        total = None
        for t in range(1, n_seq + 1):
            part = lax.dynamic_index_in_dim(parts, (s_at - t) % n_seq, 0, keepdims=False).astype(F32)
            if total is not None:
                part = part + onward(total).astype(F32)
            total = part.astype(LOW)
        return part

    def dp_sum(mine, theirs):
        if halves:
            rows = mine.shape[0] // 2
            sent = flip(low_sum(mine[rows:], theirs[rows:]), "dp", 1).astype(F32)
            return (mine[:rows].astype(F32) + theirs[:rows].astype(F32) + sent).astype(LOW)
        return lax.psum_scatter(low_sum(mine, theirs), "dp", scatter_dimension=0, tiled=True)

    near = ring_sum(dp_sum(grads[0], flip(grads[2], "mp", 1)))
    far = ring_sum(dp_sum(grads[1], flip(grads[3], "mp", 1)))
    owned = near + flip(far.astype(LOW), "mp", 2).astype(F32)
    units = up_weight.shape[1]
    up_owned, down_owned, proj_owned = owned[:, :units], owned[:, units : 2 * units], owned[:, 2 * units :]

    out_parts = share_over_mp(out_own)
    layer_out = jnp.concatenate(
        [assemble([part[b * share : (b + 1) * share] for part in out_parts], LOW) for b in range(batch)], 0
    )

    small = jnp.concatenate([sums, bias_sums], 0)
    far_small = flip(small, "mp", 2)
    common = small[:8] + far_small[:8]
    near_bias, next_bias = small[8:9] + far_small[9:10], small[10:11] + far_small[11:12]
    small = jnp.concatenate([common, next_bias], 0)
    far_small = flip(small, "mp", 1)
    small = jnp.concatenate([common + far_small[:8], near_bias + far_small[8:]], 0)

    def over_groups(value):
        for axis, size in (("dp", n_dp), ("seq", n_seq)):
            bit = 1
            while bit < size:
                value = value + flip(value, axis, bit)
                bit *= 2
        return value

    small = over_groups(small)

    gkv = token = None
    gq = q_sum = v_sum = 0.0
    input_own = []
    input_blocks = []
    lagging = []
    for b in range(batch):
        dq = None
        extra = out_t[b]
        passing = None
        for t in list(range(1, n_seq)) + [0]:
            first, last = t == 1, t == 0
            segk = seg_rows[t][b]
            if len(lagging) >= 2:
                segk = after(segk, lagging[-2])
            outs = list(
                attend_back(
                    first, last, bounds[t][b], seg_rows[0][b], segk, hidden_blocks[t][b], back[b],
                    weight_kv, queries[b], key_values[t][b], lse[b], extra, dq, gkv, weight_q,
                )
            )
            keep, send, gkv, part = outs[:4]
            v_sum = v_sum + part[0]
            if first:
                extra = outs[4]
            if last:
                gq = gq + outs[4]
                q_sum = q_sum + outs[5][0]
            else:
                dq = outs[-1]
            theirs = flip(send, "mp", 1)
            lagging.append(theirs)
            across = flip(low_sum(keep[share:], theirs[share:]), "mp", 2)
            rows = keep[:share].astype(F32) + theirs[:share].astype(F32) + across.astype(F32)
            if passing is not None:
                rows = rows + onward(passing).astype(F32)
            passing = rows.astype(LOW)
        piece = (grad_first[b * share : (b + 1) * share] + rows).astype(LOW)
        input_blocks.append(assemble(share_over_mp(piece), F32))
    input_grad = jnp.concatenate(input_blocks, 0)
    grad_qkv = jnp.concatenate([gq, gkv], 0).astype(LOW).T
    if halves:
        rows = width // 2
        parts = grad_qkv.reshape(2, rows, 3 * inner)
        mine = lax.dynamic_index_in_dim(parts, d_at, 0, keepdims=False)
        theirs = lax.dynamic_index_in_dim(parts, 1 - d_at, 0, keepdims=False)
        grad_qkv = low_sum(mine, flip(theirs, "dp", 1))
    else:
        grad_qkv = lax.psum_scatter(grad_qkv, "dp", scatter_dimension=0, tiled=True)
    qkv_owned = ring_sum(grad_qkv).reshape(shard_rows, 3, inner)
    qv_bias_grad = over_groups(jnp.stack([q_sum, v_sum]))
    return (
        layer_out,
        input_grad,
        qkv_owned,
        qv_bias_grad,
        proj_owned,
        small[3],
        small[4],
        small[5],
        up_owned,
        small[8],
        down_owned,
        small[0],
        small[1],
        small[2],
    )


def solution(mesh):
    in_specs = (
        P("dp", "seq", None),
        P("dp", "seq"),
        P("dp", "seq", None),
        P(("dp", "seq"), None, "mp"),
        P(None, "mp"),
        P(("dp", "seq"), "mp"),
        P(),
        P(),
        P(),
        P(("dp", "seq"), "mp"),
        P("mp"),
        P(("dp", "seq"), "mp"),
        P(),
        P(),
        P(),
    )
    out_specs = (
        P("dp", "seq", None),
        P("dp", "seq", None),
        P(("dp", "seq"), None, "mp"),
        P(None, "mp"),
        P(("dp", "seq"), "mp"),
        P(),
        P(),
        P(),
        P(("dp", "seq"), "mp"),
        P("mp"),
        P(("dp", "seq"), "mp"),
        P(),
        P(),
        P(),
    )
    return jax.shard_map(shards, mesh=mesh, in_specs=in_specs, out_specs=out_specs, check_vma=False)
```

time: 860 us -> 768 us (0.89); the launches traced: 843 us -> 762 us
  matrix products: 149 us -> 0 us
  starting transfers between devices: 93.3 us -> 160 us
  Pallas kernels: 108 us -> 171 us
  other arithmetic: 69.7 us -> 51.9 us
  blocking collectives: 17.3 us -> 0 us
  local copies, waits for them, and re-layouts: 200 us -> 186 us
  waiting for transfers between devices: 200 us -> 190 us
    dot_general x90 -> x0, matrix products: 149 us -> none  [dot(): lax.dot_general(left, right, dims, preferred_element_type=jnp.float32)]
    pallas_call x16 -> x21, Pallas kernels: 108 us -> 171 us  [call(): pl.pallas_call(body, out_shape=tuple(outs), in_specs=[SMEM] * scalars + [...]
    dynamic_update_slice x16 -> x17, local copies, waits for them, and re-layouts: 49.6 us -> 11.4 us  [the longest x12 8.97 us: place(): whole = lax.dynamic_update_index_in_dim(whole, piece, position, 0)]
    ppermute x27, starting transfers between devices: 14.7 us -> 47 us  [onward(): lax.ppermute(value, 'seq', [(i, (i + step) % size) for i in range(size)])]
    ppermute x70 -> x79, starting transfers between devices: 64.1 us -> 91.5 us  [flip(): return lax.ppermute(value, axis, [(i, i ^ bit) for i in range(size)])]
    ppermute x70 -> x79, waiting for transfers between devices: 117 us -> 90.3 us  [flip(): return lax.ppermute(value, axis, [(i, i ^ bit) for i in range(size)])]
    reduce_sum x23 -> x0, other arithmetic: 23.6 us -> none  [the longest x8 11.5 us: shards(): bias_v = bias_v + jnp.sum(dv, 0)]
    ppermute x0 -> x9, local copies, waits for them, and re-layouts: none -> 23.3 us  [flip(): return lax.ppermute(value, axis, [(i, i ^ bit) for i in range(size)])]
  transfers between devices with their start and end apart: 104 -> 113, of which waited for: 34 -> 36; matrix products, arithmetic and copies ran while one was open for 36% -> 21% of each run, Pallas kernels for 13% -> 17%
where the time goes in v2:
time: 768 us; the launch traced here: 762 us
  waiting for transfers between devices  190 us (25%)
  local copies, waits for them, and re-layouts  186 us (24%)
  Pallas kernels  171 us (22%)
  starting transfers between devices  160 us (21%)
  other arithmetic  51.9 us (7%)
    pallas_call x21, Pallas kernels, call(): pl.pallas_call(body, out_shape=tuple(outs), in_specs=[SMEM] * scalars + [...  171 us
    unnamed x453, local copies, waits for them, and re-layouts  92.6 us
    ppermute x79, starting transfers between devices, flip(): return lax.ppermute(value, axis, [(i, i ^ bit) for i in range(size)])  91.5 us
    ppermute x79, waiting for transfers between devices, flip(): return lax.ppermute(value, axis, [(i, i ^ bit) for i in range(size)])  90.3 us
    ppermute x27, waiting for transfers between devices, onward(): lax.ppermute(value, 'seq', [(i, (i + step) % size) for i in range(size)])  79.9 us
    ppermute x27, starting transfers between devices, onward(): lax.ppermute(value, 'seq', [(i, (i + step) % size) for i in range(size)])  47 us
    ppermute x9, local copies, waits for them, and re-layouts, flip(): return lax.ppermute(value, axis, [(i, i ^ bit) for i in range(size)])  23.3 us
    ppermute x7, starting transfers between devices, shards(): pieces.append(lax.ppermute(flat_qkv, ('dp', 'seq'), pairs))  21.7 us
  transfers between devices with their start and end apart: 113, of which 36 were waited for; matrix products, arithmetic and copies ran while one was open for 21% of the time, Pallas kernels for 17%

profile of v2, /device:TPU:0, one launch (start us, length us, event | category | flops | bytes accessed | tf_op | source)
XLA Modules:
  0.0 762.5 jit_solution(5070266199010902373)
XLA Ops:
  56.5 17.4 %collective-permute-start.46 = (bf16[384,1728]{0,1:T(8,128)(2,1)}, bf16[384,1728]{0,1:T(8,128)(2,1)}, u32[]{:S(2)}, u32[]{:S(2)}) collective-permute-start(bf16[384,1728]{0,1:T(8,128)(2,1)} %copy.91), channel_id=1, source_target_pairs={{0,2},{1,3},{2,0},{3,1},{4,6},{5,7},{6,4},{7,5},{8,10},{9,11},{10,... | collective-permute-start | bytes 3981320 | tf_op jit(solution)/shard_map/ppermute | solution.py:387
  74.1 10.8 %collective-permute-start.8 = (bf16[96,576]{0,1:T(8,128)(2,1)S(1)}, bf16[96,576]{0,1:T(8,128)(2,1)S(1)}, u32[]{:S(2)}, u32[]{:S(2)}) collective-permute-start(bf16[96,576]{0,1:T(8,128)(2,1)S(1)} %bitcast.228), channel_id=1, source_target_pairs={{0,24},{4,28},{8,16},{12,20},{16,8},{20,12},{24,0},{28,4},{1,25},{... | collective-permute-start | bytes 331784 | tf_op jit(solution)/shard_map/ppermute | solution.py:454
  84.9 14.3 %collective-permute-done.8 = bf16[96,576]{0,1:T(8,128)(2,1)S(1)} collective-permute-done((bf16[96,576]{0,1:T(8,128)(2,1)S(1)}, bf16[96,576]{0,1:T(8,128)(2,1)S(1)}, u32[]{:S(2)}, u32[]{:S(2)}) %collective-permute-start.8) | collective-permute-done | bytes 110624 | tf_op jit(solution)/shard_map/ppermute | solution.py:454
  108.8 9.9 %collective-permute-done.15.refs_1_ = bf16[256,768]{1,0:T(8,128)(2,1)} collective-permute-done((bf16[256,768]{1,0:T(8,128)(2,1)}, bf16[256,768]{1,0:T(8,128)(2,1)}, u32[]{:S(2)}, u32[]{:S(2)}) %collective-permute-start.15) | collective-permute-done | bytes 393248 | tf_op jit(solution)/shard_map/ppermute | solution.py:387
  137.5 10.7 %collective-permute-done.29.refs_0_ = bf16[256,768]{1,0:T(8,128)(2,1)} collective-permute-done((bf16[256,768]{1,0:T(8,128)(2,1)S(1)}, bf16[256,768]{1,0:T(8,128)(2,1)}, u32[]{:S(2)}, u32[]{:S(2)}) %collective-permute-start.29) | collective-permute-done | bytes 393248 | tf_op jit(solution)/shard_map/ppermute | solution.py:392
  156.1 8.4 %collective-permute-done.26.refs_1_ = bf16[256,768]{1,0:T(8,128)(2,1)} collective-permute-done((bf16[256,768]{1,0:T(8,128)(2,1)}, bf16[256,768]{1,0:T(8,128)(2,1)}, u32[]{:S(2)}, u32[]{:S(2)}) %collective-permute-start.26) | collective-permute-done | bytes 393248 | tf_op jit(solution)/shard_map/ppermute | solution.py:387
  181.3 11.4 %collective-permute-done.50 = bf16[384,1728]{0,1:T(8,128)(2,1)} collective-permute-done((bf16[384,1728]{0,1:T(8,128)(2,1)}, bf16[384,1728]{0,1:T(8,128)(2,1)}, u32[]{:S(2)}, u32[]{:S(2)}) %collective-permute-start.50) | collective-permute-done | bytes 1327136 | tf_op jit(solution)/shard_map/ppermute | solution.py:387
  210.4 9.3 %shard_map.254 = (bf16[1024,384]{1,0:T(8,128)(2,1)S(1)}, bf16[1024,192]{1,0:T(8,128)(2,1)S(1)}, f32[8,1024]{1,0:T(8,128)S(1)}, f32[8,1024]{1,0:T(8,128)S(1)}, f32[192,1024]{1,0:T(8,128)S(1)}) custom-call(s32[4,2]{1,0:T(4,128)S(1)} %get-tuple-element.405.bounds, f32[1,1024]{1,0:T(1,128)S(1)} %get-tuple-element.194.segq.segk, ...), custom_call_target="tpu_custom_call" | custom-call | tf_op jit(solution)/shard_map/pallas_call | solution.py:35
  220.6 9.1 %shard_map.255 = (bf16[1024,384]{1,0:T(8,128)(2,1)S(1)}, bf16[1024,192]{1,0:T(8,128)(2,1)S(1)}, f32[8,1024]{1,0:T(8,128)S(1)}, f32[8,1024]{1,0:T(8,128)S(1)}, f32[192,1024]{1,0:T(8,128)S(1)}) custom-call(s32[4,2]{1,0:T(4,128)S(1)} %get-tuple-element.404.bounds, f32[1,1024]{1,0:T(1,128)S(1)} %add_convert_fusion.25.segq.segk, ...), custom_call_target="tpu_custom_call" | custom-call | tf_op jit(solution)/shard_map/pallas_call | solution.py:35
  230.7 9.3 %shard_map.256 = (bf16[1024,384]{1,0:T(8,128)(2,1)S(1)}, f32[8,1024]{1,0:T(8,128)S(1)}, f32[8,1024]{1,0:T(8,128)S(1)}, f32[192,1024]{1,0:T(8,128)S(1)}) custom-call(s32[4,2]{1,0:T(4,128)S(1)} %get-tuple-element.407.bounds, f32[1,1024]{1,0:T(1,128)S(1)} %get-tuple-element.194.segq.segk, f32[1,1024]{1,0:T(1,128)S(1)} %add_convert_fusion.24.segk, ...), custom_call_target="tpu_custom_call" | custom-call | tf_op jit(solution)/shard_map/pallas_call | solution.py:35
  240.6 9.9 %shard_map.257 = (bf16[1024,384]{1,0:T(8,128)(2,1)S(1)}, f32[8,1024]{1,0:T(8,128)S(1)}, f32[8,1024]{1,0:T(8,128)S(1)}, f32[192,1024]{1,0:T(8,128)S(1)}) custom-call(s32[4,2]{1,0:T(4,128)S(1)} %get-tuple-element.406.bounds, f32[1,1024]{1,0:T(1,128)S(1)} %get-tuple-element.194.segq.segk, f32[1,1024]{1,0:T(1,128)S(1)} %get-tuple-element.148.segk, ...), custom_call_target="tpu_custom_call" | custom-call | tf_op jit(solution)/shard_map/pallas_call | solution.py:35
  252.1 9.7 %shard_map.258 = (bf16[1024,384]{1,0:T(8,128)(2,1)S(1)}, bf16[256,192]{1,0:T(8,128)(2,1)S(1)}, bf16[256,192]{1,0:T(8,128)(2,1)S(1)}, bf16[256,192]{1,0:T(8,128)(...) custom-call(s32[4,2]{1,0:T(4,128)S(1)} %get-tuple-element.408.bounds, ...), custom_call_target="tpu_custom_call" | custom-call | tf_op jit(solution)/shard_map/pallas_call | solution.py:35
  318.4 26.2 %shard_map.262 = (bf16[512,768]{1,0:T(8,128)(2,1)S(1)}, f32[512,768]{1,0:T(8,128)}, f32[8,768]{1,0:T(8,128)S(1)}, f32[4,768]{1,0:T(4,128)S(1)}, bf16[256,192]{1,...) custom-call(s32[1]{0:T(128)} %bitcast.flag, ...), custom_call_target="tpu_custom_call" | custom-call | tf_op jit(solution)/shard_map/pallas_call | solution.py:35
  365.5 12.7 %shard_map.263 = (bf16[512,768]{1,0:T(8,128)(2,1)S(1)}, bf16[512,768]{1,0:T(8,128)(2,1)}, f32[384,768]{1,0:T(8,128)S(1)}, f32[8,192]{1,0:T(8,128)S(1)}, f32[8,1024]{1,0:T(8,128)S(1)}, /*index=5*/f32[192,1024]{1,0:T(8,128)S(1)}) custom-call(s32[4,2]{1,0:T(4,128)S(1)} %copy-done.161, f32[1,1024]{1,0:T(1,128)S(1)} %get-tuple-element.194.segq.segk, ...), custom_call_target="tpu_custom_call" | custom-call | tf_op jit(solution)/shard_map/pallas_call | solution.py:35
  390.6 18.1 %collective-permute-start.111 = (f32[9,768]{1,0:T(8,128)S(1)}, f32[9,768]{1,0:T(8,128)S(1)}, u32[]{:S(2)}, u32[]{:S(2)}) collective-permute-start(f32[9,768]{1,0:T(8,128)S(1)} %fusion.15), channel_id=1, source_target_pairs={{0,4},{4,0},{8,12},{12,8},{1,5},{5,1},{9,13},{13,9},{2,6},{6,2},{1... | collective-permute-start | bytes 82952 | tf_op jit(solution)/shard_map/ppermute | solution.py:387
  418.0 12.3 %shard_map.264 = (bf16[512,768]{1,0:T(8,128)(2,1)S(1)}, bf16[512,768]{1,0:T(8,128)(2,1)}, f32[384,768]{1,0:T(8,128)S(1)}, f32[8,192]{1,0:T(8,128)S(1)}, f32[192,1024]{1,0:T(8,128)S(1)}) custom-call(s32[4,2]{1,0:T(4,128)S(1)} %copy-done.159, f32[1,1024]{1,0:T(1,128)S(1)} %get-tuple-element.194.segq.segk, f32[1,1024]{1,0:T(1,128)S(1)} %copy-done.149, ...), custom_call_target="tpu_custom_call" | custom-call | tf_op jit(solution)/shard_map/pallas_call | solution.py:35
  471.1 12.2 %shard_map.265 = (bf16[512,768]{1,0:T(8,128)(2,1)S(1)}, bf16[512,768]{1,0:T(8,128)(2,1)S(1)}, f32[384,768]{1,0:T(8,128)S(1)}, f32[8,192]{1,0:T(8,128)S(1)}, f32[192,1024]{1,0:T(8,128)S(1)}) custom-call(s32[4,2]{1,0:T(4,128)S(1)} %copy-done.157, f32[1,1024]{1,0:T(1,128)S(1)} %get-tuple-element.194.segq.segk, f32[1,1024]{1,0:T(1,128)S(1)} %copy-done.145, ...), custom_call_target="tpu_custom_call" | custom-call | tf_op jit(solution)/shard_map/pallas_call | solution.py:35
  484.1 12.3 %shard_map.266 = (bf16[512,768]{1,0:T(8,128)(2,1)S(1)}, bf16[512,768]{1,0:T(8,128)(2,1)S(1)}, f32[384,768]{1,0:T(8,128)S(1)}, f32[8,192]{1,0:T(8,128)S(1)}, f32[...) custom-call(s32[4,2]{1,0:T(4,128)S(1)} %copy-done.165, f32[1,1024]{1,0:T(1,128)S(1)} %get-tuple-element.194.segq.segk, ...), custom_call_target="tpu_custom_call" | custom-call | tf_op jit(solution)/shard_map/pallas_call | solution.py:35
  530.8 14.1 %collective-permute-start.69 = (bf16[256,768]{1,0:T(8,128)(2,1)S(1)}, bf16[256,768]{1,0:T(8,128)(2,1)S(1)}, u32[]{:S(2)}, u32[]{:S(2)}) collective-permute-start(bf16[256,768]{1,0:T(8,128)(2,1)S(1)} %add_convert_fusion.13), channel_id=1, source_target_pairs={{0,4},{4,8},{8,12},{12,0},{1,5},{5,9},{9,13},{13,1},{2,6},{6,10},{... | collective-permute-start | bytes 1179656 | tf_op jit(solution)/shard_map/ppermute | solution.py:392
  546.9 12.1 %collective-permute-done.69 = bf16[256,768]{1,0:T(8,128)(2,1)S(1)} collective-permute-done((bf16[256,768]{1,0:T(8,128)(2,1)S(1)}, bf16[256,768]{1,0:T(8,128)(2,1)S(1)}, u32[]{:S(2)}, u32[]{:S(2)}) %collective-permute-start.69) | collective-permute-done | bytes 393248 | tf_op jit(solution)/shard_map/ppermute | solution.py:392
  573.4 12.6 %shard_map.270 = (bf16[512,768]{1,0:T(8,128)(2,1)S(1)}, bf16[512,768]{1,0:T(8,128)(2,1)}, f32[384,768]{1,0:T(8,128)S(1)}, f32[8,192]{1,0:T(8,128)S(1)}, f32[192,768]{1,0:T(8,128)S(1)}, /*index=5*/f32[8,192]{1,0:T(8,128)S(1)}) custom-call(s32[4,2]{1,0:T(4,128)S(1)} %copy-done.163, f32[1,1024]{1,0:T(1,128)S(1)} %add_convert_fusion.25.segq.segk, ...), custom_call_target="tpu_custom_call" | custom-call | tf_op jit(solution)/shard_map/pallas_call | solution.py:35
  692.2 17.9 %collective-permute-done.103 = bf16[384,1728]{0,1:T(8,128)(2,1)} collective-permute-done((bf16[384,1728]{0,1:T(8,128)(2,1)}, bf16[384,1728]{0,1:T(8,128)(2,1)}, u32[]{:S(2)}, u32[]{:S(2)}) %collective-permute-start.103) | collective-permute-done | bytes 1327136 | tf_op jit(solution)/shard_map/ppermute | solution.py:387
  726.5 13.3 %collective-permute-done.105 = bf16[96,1728]{1,0:T(8,128)(2,1)S(1)} collective-permute-done((bf16[96,1728]{1,0:T(8,128)(2,1)S(1)}, bf16[96,1728]{1,0:T(8,128)(2,1)S(1)}, u32[]{:S(2)}, u32[]{:S(2)}) %collective-permute-start.105) | collective-permute-done | bytes 331808 | tf_op jit(solution)/shard_map/ppermute | solution.py:392
  740.2 12.6 %collective-permute-done.106 = bf16[96,1728]{1,0:T(8,128)(2,1)S(1)} collective-permute-done((bf16[96,1728]{1,0:T(8,128)(2,1)S(1)}, bf16[96,1728]{1,0:T(8,128)(2,1)S(1)}, u32[]{:S(2)}, u32[]{:S(2)}) %collective-permute-start.106) | collective-permute-done | bytes 331808 | tf_op jit(solution)/shard_map/ppermute | solution.py:392
  (861 shorter events, 452.1 us)
Async XLA Ops:
  5.7 38.9 %collective-permute-start.2 = (s32[2,1024]{1,0:T(2,128)}, s32[2,1024]{1,0:T(2,128)S(1)}, u32[]{:S(2)}, u32[]{:S(2)}) collective-permute-start(s32[2,1024]{1,0:T(2,128)} %param.16), channel_id=1, source_target_pairs={{0,4},{4,8},{8,12},{12,0},{1,5},{5,9},{9,13},{13,1},{2,6},{6,10},{... | collective-permute-start | bytes 24584 | tf_op jit(solution)/shard_map/ppermute | solution.py:392
  52.5 53.8 %collective-permute-start.14 = (bf16[256,768]{1,0:T(8,128)(2,1)S(1)}, bf16[256,768]{1,0:T(8,128)(2,1)}, u32[]{:S(2)}, u32[]{:S(2)}) collective-permute-start(bf16[256,768]{1,0:T(8,128)(2,1)S(1)} %get-tuple-element.356.refs_0_), channel_id=1, source_target_pairs={{0,8},{4,12},{8,0},{12,4},{1,9},{5,13},{9,1},{13,5},{2,10},{6,14},... | collective-permute-start | bytes 1179656 | tf_op jit(solution)/shard_map/ppermute | solution.py:392
  54.5 52.9 %collective-permute-start.18 = (bf16[256,768]{1,0:T(8,128)(2,1)S(1)}, bf16[256,768]{1,0:T(8,128)(2,1)}, u32[]{:S(2)}, u32[]{:S(2)}) collective-permute-start(bf16[256,768]{1,0:T(8,128)(2,1)S(1)} %get-tuple-element.356.refs_0_), channel_id=1, source_target_pairs={{0,12},{4,0},{8,4},{12,8},{1,13},{5,1},{9,5},{13,9},{2,14},{6,2},{... | collective-permute-start | bytes 1179656 | tf_op jit(solution)/shard_map/ppermute | solution.py:392
  56.5 93.9 %collective-permute-start.46 = (bf16[384,1728]{0,1:T(8,128)(2,1)}, bf16[384,1728]{0,1:T(8,128)(2,1)}, u32[]{:S(2)}, u32[]{:S(2)}) collective-permute-start(bf16[384,1728]{0,1:T(8,128)(2,1)} %copy.91), channel_id=1, source_target_pairs={{0,2},{1,3},{2,0},{3,1},{4,6},{5,7},{6,4},{7,5},{8,10},{9,11},{10,... | collective-permute-start | bytes 3981320 | tf_op jit(solution)/shard_map/ppermute | solution.py:387
  135.9 45.3 %collective-permute-start.49 = (bf16[384,1728]{0,1:T(8,128)(2,1)}, bf16[384,1728]{0,1:T(8,128)(2,1)}, u32[]{:S(2)}, u32[]{:S(2)}) collective-permute-start(bf16[384,1728]{0,1:T(8,128)(2,1)} %copy.91), channel_id=1, source_target_pairs={{0,16},{16,0},{1,17},{17,1},{2,18},{18,2},{3,19},{19,3},{4,20},{20... | collective-permute-start | bytes 3981320 | tf_op jit(solution)/shard_map/ppermute | solution.py:387
  150.4 42.3 %collective-permute-start.50 = (bf16[384,1728]{0,1:T(8,128)(2,1)}, bf16[384,1728]{0,1:T(8,128)(2,1)}, u32[]{:S(2)}, u32[]{:S(2)}) collective-permute-start(bf16[384,1728]{0,1:T(8,128)(2,1)} %collective-permute-done.46), channel_id=1, source_target_pairs={{0,16},{16,0},{1,17},{17,1},{2,18},{18,2},{3,19},{19,3},{4,20},{20... | collective-permute-start | bytes 3981320 | tf_op jit(solution)/shard_map/ppermute | solution.py:387
  180.7 102.2 %collective-permute-start.47 = (bf16[384,1728]{0,1:T(8,128)(2,1)}, bf16[384,1728]{0,1:T(8,128)(2,1)}, u32[]{:S(2)}, u32[]{:S(2)}) collective-permute-start(bf16[384,1728]{0,1:T(8,128)(2,1)} %copy.91), channel_id=1, source_target_pairs={{0,1},{1,0},{2,3},{3,2},{4,5},{5,4},{6,7},{7,6},{8,9},{9,8},{10,11... | collective-permute-start | bytes 3981320 | tf_op jit(solution)/shard_map/ppermute | solution.py:387
  180.7 102.6 %collective-permute-start.48 = (bf16[384,1728]{0,1:T(8,128)(2,1)}, bf16[384,1728]{0,1:T(8,128)(2,1)}, u32[]{:S(2)}, u32[]{:S(2)}) collective-permute-start(bf16[384,1728]{0,1:T(8,128)(2,1)} %collective-permute-done.46), channel_id=1, source_target_pairs={{0,1},{1,0},{2,3},{3,2},{4,5},{5,4},{6,7},{7,6},{8,9},{9,8},{10,11... | collective-permute-start | bytes 3981320 | tf_op jit(solution)/shard_map/ppermute | solution.py:387
  181.2 103.6 %collective-permute-start.51 = (bf16[384,1728]{0,1:T(8,128)(2,1)}, bf16[384,1728]{0,1:T(8,128)(2,1)}, u32[]{:S(2)}, u32[]{:S(2)}) collective-permute-start(bf16[384,1728]{0,1:T(8,128)(2,1)} %collective-permute-done.49), channel_id=1, source_target_pairs={{0,1},{1,0},{2,3},{3,2},{4,5},{5,4},{6,7},{7,6},{8,9},{9,8},{10,11... | collective-permute-start | bytes 3981320 | tf_op jit(solution)/shard_map/ppermute | solution.py:387
  192.7 92.2 %collective-permute-start.52 = (bf16[384,1728]{0,1:T(8,128)(2,1)}, bf16[384,1728]{0,1:T(8,128)(2,1)}, u32[]{:S(2)}, u32[]{:S(2)}) collective-permute-start(bf16[384,1728]{0,1:T(8,128)(2,1)} %collective-permute-done.50), channel_id=1, source_target_pairs={{0,1},{1,0},{2,3},{3,2},{4,5},{5,4},{6,7},{7,6},{8,9},{9,8},{10,11... | collective-permute-start | bytes 3981320 | tf_op jit(solution)/shard_map/ppermute | solution.py:387
  199.9 65.0 %collective-permute-start.36 = (bf16[256,768]{1,0:T(8,128)(2,1)}, bf16[256,768]{1,0:T(8,128)(2,1)}, u32[]{:S(2)}, u32[]{:S(2)}) collective-permute-start(bf16[256,768]{1,0:T(8,128)(2,1)} %collective-permute-done.34.refs_1_), channel_id=1, source_target_pairs={{0,1},{1,0},{2,3},{3,2},{4,5},{5,4},{6,7},{7,6},{8,9},{9,8},{10,11... | collective-permute-start | bytes 1179656 | tf_op jit(solution)/shard_map/ppermute | solution.py:387
  381.7 52.8 %collective-permute-start.60 = (bf16[512,768]{1,0:T(8,128)(2,1)}, bf16[512,768]{1,0:T(8,128)(2,1)}, u32[]{:S(2)}, u32[]{:S(2)}) collective-permute-start(bf16[512,768]{1,0:T(8,128)(2,1)} %get-tuple-element.195), channel_id=1, source_target_pairs={{0,1},{1,0},{2,3},{3,2},{4,5},{5,4},{6,7},{7,6},{8,9},{9,8},{10,11... | collective-permute-start | bytes 2359304 | tf_op jit(solution)/shard_map/ppermute | solution.py:387
  387.3 112.7 %collective-permute-start.53 = (bf16[512,768]{1,0:T(8,128)(2,1)}, bf16[512,768]{1,0:T(8,128)(2,1)}, u32[]{:S(2)}, u32[]{:S(2)}) collective-permute-start(bf16[512,768]{1,0:T(8,128)(2,1)} %copy-done.57), channel_id=1, source_target_pairs={{0,2},{1,3},{2,0},{3,1},{4,6},{5,7},{6,4},{7,5},{8,10},{9,11},{10,... | collective-permute-start | bytes 2359304 | tf_op jit(solution)/shard_map/ppermute | solution.py:387
  388.8 127.5 %collective-permute-start.54 = (bf16[512,768]{1,0:T(8,128)(2,1)}, bf16[512,768]{1,0:T(8,128)(2,1)}, u32[]{:S(2)}, u32[]{:S(2)}) collective-permute-start(bf16[512,768]{1,0:T(8,128)(2,1)} %copy-done.57), channel_id=1, source_target_pairs={{0,1},{1,0},{2,3},{3,2},{4,5},{5,4},{6,7},{7,6},{8,9},{9,8},{10,11... | collective-permute-start | bytes 2359304 | tf_op jit(solution)/shard_map/ppermute | solution.py:387
  390.6 41.5 %collective-permute-start.111 = (f32[9,768]{1,0:T(8,128)S(1)}, f32[9,768]{1,0:T(8,128)S(1)}, u32[]{:S(2)}, u32[]{:S(2)}) collective-permute-start(f32[9,768]{1,0:T(8,128)S(1)} %fusion.15), channel_id=1, source_target_pairs={{0,4},{4,0},{8,12},{12,8},{1,5},{5,1},{9,13},{13,9},{2,6},{6,2},{1... | collective-permute-start | bytes 82952 | tf_op jit(solution)/shard_map/ppermute | solution.py:387
  430.4 53.6 %collective-permute-start.59 = (bf16[512,768]{1,0:T(8,128)(2,1)}, bf16[512,768]{1,0:T(8,128)(2,1)}, u32[]{:S(2)}, u32[]{:S(2)}) collective-permute-start(bf16[512,768]{1,0:T(8,128)(2,1)} %get-tuple-element.193), channel_id=1, source_target_pairs={{0,1},{1,0},{2,3},{3,2},{4,5},{5,4},{6,7},{7,6},{8,9},{9,8},{10,11... | collective-permute-start | bytes 2359304 | tf_op jit(solution)/shard_map/ppermute | solution.py:387
  436.6 61.6 %collective-permute-start.66 = (bf16[256,768]{1,0:T(8,128)(2,1)}, bf16[256,768]{1,0:T(8,128)(2,1)}, u32[]{:S(2)}, u32[]{:S(2)}) collective-permute-start(bf16[256,768]{1,0:T(8,128)(2,1)} %add_convert_fusion.16), channel_id=1, source_target_pairs={{0,2},{1,3},{2,0},{3,1},{4,6},{5,7},{6,4},{7,5},{8,10},{9,11},{10,... | collective-permute-start | bytes 1179656 | tf_op jit(solution)/shard_map/ppermute | solution.py:387
  519.5 85.1 %collective-permute-start.97 = (bf16[768,1728]{0,1:T(8,128)(2,1)}, bf16[768,1728]{0,1:T(8,128)(2,1)}, u32[]{:S(2)}, u32[]{:S(2)}) collective-permute-start(bf16[768,1728]{0,1:T(8,128)(2,1)} %copy.105), channel_id=1, source_target_pairs={{0,1},{1,0},{2,3},{3,2},{4,5},{5,4},{6,7},{7,6},{8,9},{9,8},{10,11... | collective-permute-start | bytes 7962632 | tf_op jit(solution)/shard_map/ppermute | solution.py:387
  546.9 63.3 %collective-permute-start.102 = (bf16[768,1728]{0,1:T(8,128)(2,1)}, bf16[768,1728]{0,1:T(8,128)(2,1)}, u32[]{:S(2)}, u32[]{:S(2)}) collective-permute-start(bf16[768,1728]{0,1:T(8,128)(2,1)} %copy.110), channel_id=1, source_target_pairs={{0,1},{1,0},{2,3},{3,2},{4,5},{5,4},{6,7},{7,6},{8,9},{9,8},{10,11... | collective-permute-start | bytes 7962632 | tf_op jit(solution)/shard_map/ppermute | solution.py:387
  561.5 84.1 %collective-permute-start.70 = (bf16[256,768]{1,0:T(8,128)(2,1)}, bf16[256,768]{1,0:T(8,128)(2,1)}, u32[]{:S(2)}, u32[]{:S(2)}) collective-permute-start(bf16[256,768]{1,0:T(8,128)(2,1)} %get-tuple-element.338), channel_id=1, source_target_pairs={{0,2},{1,3},{2,0},{3,1},{4,6},{5,7},{6,4},{7,5},{8,10},{9,11},{10,... | collective-permute-start | bytes 1179656 | tf_op jit(solution)/shard_map/ppermute | solution.py:387
  562.1 90.6 %collective-permute-start.71 = (bf16[256,768]{1,0:T(8,128)(2,1)}, bf16[256,768]{1,0:T(8,128)(2,1)}, u32[]{:S(2)}, u32[]{:S(2)}) collective-permute-start(bf16[256,768]{1,0:T(8,128)(2,1)} %get-tuple-element.338), channel_id=1, source_target_pairs={{0,1},{1,0},{2,3},{3,2},{4,5},{5,4},{6,7},{7,6},{8,9},{9,8},{10,11... | collective-permute-start | bytes 1179656 | tf_op jit(solution)/shard_map/ppermute | solution.py:387
  604.6 66.9 %collective-permute-start.78 = (bf16[512,768]{1,0:T(8,128)(2,1)}, bf16[512,768]{1,0:T(8,128)(2,1)}, u32[]{:S(2)}, u32[]{:S(2)}) collective-permute-start(bf16[512,768]{1,0:T(8,128)(2,1)} %get-tuple-element.229), channel_id=1, source_target_pairs={{0,1},{1,0},{2,3},{3,2},{4,5},{5,4},{6,7},{7,6},{8,9},{9,8},{10,11... | collective-permute-start | bytes 2359304 | tf_op jit(solution)/shard_map/ppermute | solution.py:387
  663.8 46.3 %collective-permute-start.103 = (bf16[384,1728]{0,1:T(8,128)(2,1)}, bf16[384,1728]{0,1:T(8,128)(2,1)}, u32[]{:S(2)}, u32[]{:S(2)}) collective-permute-start(bf16[384,1728]{0,1:T(8,128)(2,1)} %copy.113), channel_id=1, source_target_pairs={{0,16},{16,0},{1,17},{17,1},{2,18},{18,2},{3,19},{19,3},{4,20},{20... | collective-permute-start | bytes 3981320 | tf_op jit(solution)/shard_map/ppermute | solution.py:387
  672.8 42.3 %collective-permute-start.79 = (bf16[256,768]{1,0:T(8,128)(2,1)S(1)}, bf16[256,768]{1,0:T(8,128)(2,1)S(1)}, u32[]{:S(2)}, u32[]{:S(2)}) collective-permute-start(bf16[256,768]{1,0:T(8,128)(2,1)S(1)} %add_convert_fusion.11), channel_id=1, source_target_pairs={{0,2},{1,3},{2,0},{3,1},{4,6},{5,7},{6,4},{7,5},{8,10},{9,11},{10,... | collective-permute-start | bytes 1179656 | tf_op jit(solution)/shard_map/ppermute | solution.py:387
  (311 other events, 4788.7 us)
